TPU v7x, 512 devices: a whole 4x8x8 slice. The times are simulated.
512 devices in a mesh: patch: 128 (over y, z, core), lat: 4 (over x).
Axes of the slice: x: 4, y: 8, z: 8, core: 2. Of those that a mesh axis runs over, the one named last changes fastest.
Arguments:
- nodes: bfloat16 [32768, 512], P('patch', 'lat'), may hold values from -6 to 6
- short_edges: bfloat16 [131072, 512], P(('patch', 'lat')), may hold values from -6 to 6
- long_edges: bfloat16 [65536, 512], P(('patch', 'lat')), may hold values from -6 to 6
- short_send: int32 [131072], P(('patch', 'lat')), may hold values from 0 to 511
- short_recv: int32 [131072], P(('patch', 'lat')), may hold values from 0 to 63
- long_send: int32 [65536], P(('patch', 'lat')), may hold values from 0 to 255
- long_recv: int32 [65536], P(('patch', 'lat')), may hold values from 0 to 63
- send_rows: int32 [128, 128, 2], P('patch'), may hold values from 0 to 15
- tile_rows: int32 [128, 128, 2], P('patch'), may hold values from 0 to 255
- edge_w_in: bfloat16 [1536, 512], replicated, may hold values from -0.15625 to 0.15625
- edge_b_in: float32 [512], replicated, may hold values from -3 to 3
- edge_w_out: bfloat16 [512, 512], replicated, may hold values from -0.25 to 0.25
- edge_b_out: float32 [512], replicated, may hold values from -3 to 3
- edge_gain: float32 [512], replicated, may hold values from 0.5 to 1.5
- edge_shift: float32 [512], replicated, may hold values from -3 to 3
- node_w_in: bfloat16 [1024, 512], replicated, may hold values from -0.1875 to 0.1875
- node_b_in: float32 [512], replicated, may hold values from -3 to 3
- node_w_out: bfloat16 [512, 512], replicated, may hold values from -0.25 to 0.25
- node_b_out: float32 [512], replicated, may hold values from -3 to 3
- node_gain: float32 [512], replicated, may hold values from 0.5 to 1.5
- node_shift: float32 [512], replicated, may hold values from -3 to 3
Outputs:
- short_new: bfloat16 [131072, 512], P(('patch', 'lat'))
- long_new: bfloat16 [65536, 512], P(('patch', 'lat'))
- new_nodes: bfloat16 [32768, 512], P('patch', 'lat')
- tiles: bfloat16 [32768, 512], P('patch', 'lat')
Inputs may be any that keep to these rules, and one draw needn't show every extreme that they name: `send_rows`: coarse rows are the first 16 rows of a patch.
All inputs are finite; a program needn't handle non-finite values.
Results may differ from a plain program's by a relative error of at most 0.005.
Values may be sent and summed in bfloat16 or wider, within the bound.
No kernel may reach another device: no remote copies, remote signals or barrier semaphores. Data moves between devices by JAX's collectives and lax.ppermute only.
A program may use at most 64 MiB of HBM per device.

v0:
```python
import jax
import jax.numpy as jnp
from jax import lax
from jax.sharding import PartitionSpec as P

HALO = 128


def with_halo(array, sides, width):
    for axis, dim in sides:
        count, length = (lax.axis_size(axis), array.shape[dim])
        up = [(i, (i + 1) % count) for i in range(count)]
        down = [(j, i) for i, j in up]
        last = lax.slice_in_dim(array, length - width, length, axis=dim)
        initial = lax.slice_in_dim(array, 0, width, axis=dim)
        before = lax.ppermute(last, axis, up)
        after = lax.ppermute(initial, axis, down)
        array = jnp.concatenate([before, array, after], axis=dim)
    return array


def norm_rows(values, gain_row, shift_row):
    average = jnp.mean(values, axis=-1, keepdims=True)
    centered = values - average
    variance = jnp.mean(centered * centered, axis=-1, keepdims=True)
    return centered * lax.rsqrt(variance + 1e-05) * gain_row + shift_row


def body(
    nodes,
    short_edges,
    long_edges,
    short_send,
    short_recv,
    long_send,
    long_recv,
    send_rows,
    tile_rows,
    edge_w_in,
    edge_b_in,
    edge_w_out,
    edge_b_out,
    edge_gain,
    edge_shift,
    node_w_in,
    node_b_in,
    node_w_out,
    node_b_out,
    node_gain,
    node_shift,
):
    latent = edge_w_out.shape[0]
    node_count = nodes.shape[0]
    patches = lax.axis_size("patch")
    full_rows = lax.all_gather(nodes, "lat", axis=1, tiled=True)
    haloed = with_halo(full_rows, (("patch", 0),), HALO)
    slot_count = send_rows.shape[2]
    outgoing = jnp.take(full_rows, send_rows[0].reshape(-1), axis=0).reshape(
        patches, slot_count, latent
    )
    arrived = lax.all_to_all(outgoing, "patch", split_axis=0, concat_axis=0, tiled=True).reshape(
        patches * slot_count, latent
    )
    quarter = node_count // lax.axis_size("lat")
    own_rows = lax.dynamic_slice_in_dim(full_rows, lax.axis_index("lat") * quarter, quarter, 0)
    sent_near = jnp.dot(haloed, edge_w_in[latent : 2 * latent], preferred_element_type=jnp.float32)
    sent_far = jnp.dot(arrived, edge_w_in[latent : 2 * latent], preferred_element_type=jnp.float32)
    recv_proj = jnp.dot(own_rows, edge_w_in[2 * latent :], preferred_element_type=jnp.float32)
    short_count = short_edges.shape[0]
    all_edges = jnp.concatenate([short_edges, long_edges], axis=0)
    extra = jnp.concatenate(
        [
            jnp.take(sent_near, short_send, axis=0) + jnp.take(recv_proj, short_recv, axis=0),
            jnp.take(sent_far, long_send, axis=0) + jnp.take(recv_proj, long_recv, axis=0),
        ],
        axis=0,
    )
    before = (
        jnp.dot(all_edges, edge_w_in[:latent], preferred_element_type=jnp.float32)
        + extra
        + edge_b_in
    )
    hidden = jax.nn.silu(before).astype(jnp.bfloat16)
    output = jnp.dot(hidden, edge_w_out, preferred_element_type=jnp.float32) + edge_b_out
    updated = (all_edges.astype(jnp.float32) + norm_rows(output, edge_gain, edge_shift)).astype(
        jnp.bfloat16
    )
    receivers = jnp.concatenate([short_recv, long_recv], axis=0)
    one_hot = (receivers[None, :] == jnp.arange(quarter, dtype=jnp.int32)[:, None]).astype(
        jnp.bfloat16
    )
    aggregate = jnp.dot(one_hot, updated, preferred_element_type=jnp.float32).astype(jnp.bfloat16)
    node_before = jnp.dot(own_rows, node_w_in[:latent], preferred_element_type=jnp.float32)
    node_before = (
        node_before
        + jnp.dot(aggregate, node_w_in[latent:], preferred_element_type=jnp.float32)
        + node_b_in
    )
    node_hidden = jax.nn.silu(node_before).astype(jnp.bfloat16)
    node_output = jnp.dot(node_hidden, node_w_out, preferred_element_type=jnp.float32) + node_b_out
    updated_own = (
        own_rows.astype(jnp.float32) + norm_rows(node_output, node_gain, node_shift)
    ).astype(jnp.bfloat16)
    node_rows = lax.all_to_all(updated_own, "lat", split_axis=1, concat_axis=0, tiled=True)
    tile_slots = tile_rows.shape[2]
    tile_send = jnp.take(node_rows, tile_rows[0].reshape(-1), axis=0).reshape(
        patches, tile_slots, node_rows.shape[1]
    )
    tiles = lax.all_to_all(tile_send, "patch", split_axis=0, concat_axis=0, tiled=True).reshape(
        patches * tile_slots, node_rows.shape[1]
    )
    return (updated[:short_count], updated[short_count:], node_rows, tiles)


def solution(mesh):
    placed = (
        P("patch", "lat"),
        P(("patch", "lat"), None),
        P(("patch", "lat"), None),
        P(("patch", "lat")),
        P(("patch", "lat")),
        P(("patch", "lat")),
        P(("patch", "lat")),
        P("patch", None, None),
        P("patch", None, None),
        P(),
        P(),
        P(),
        P(),
        P(),
        P(),
        P(),
        P(),
        P(),
        P(),
        P(),
        P(),
    )
    return jax.shard_map(
        body,
        mesh=mesh,
        in_specs=placed,
        out_specs=(
            P(("patch", "lat"), None),
            P(("patch", "lat"), None),
            P("patch", "lat"),
            P("patch", "lat"),
        ),
        check_vma=False,
    )
```

profile of v0, /device:TPU:1, one launch (start us, length us, event | category | flops | bytes accessed | tf_op | source)
XLA Modules:
  0.0 96.4 jit_solution(8475849892961313332)
XLA Ops:
  0.6 0.0 copy-start
  0.6 10.6 %all_gather.3 = bf16[256,512]{1,0:T(8,128)(2,1)S(1)} all-gather(bf16[256,128]{1,0:T(8,128)(2,1)} %param.21), channel_id=1, replica_groups=mesh['patch'=128,'lat'=4] {'lat'}, dimensions={1}, use_global_device_ids=true | all-gather | bytes 327680 | tf_op jit(solution)/shard_map/all_gather | solution.py:55
  11.3 7.2 %collective-permute-start = (bf16[128,512]{1,0:T(8,128)(2,1)S(1)}, bf16[128,512]{1,0:T(8,128)(2,1)}, u32[]{:S(2)}, u32[]{:S(2)}) collective-permute-start(bf16[128,512]{1,0:T(8,128)(2,1)S(1)} %get-tuple-element.4), channel_id=1, source_target_pairs={{0,4},{4,8},{8,12},{12,16},{16,20},{20,24},{24,28},{28,32},{32,36}... | collective-permute-start | bytes 393224 | tf_op jit(solution)/shard_map/ppermute | solution.py:16
  18.5 4.4 %collective-permute-start.1 = (bf16[128,512]{1,0:T(8,128)(2,1)S(1)}, bf16[128,512]{1,0:T(8,128)(2,1)}, u32[]{:S(2)}, u32[]{:S(2)}) collective-permute-start(bf16[128,512]{1,0:T(8,128)(2,1)S(1)} %get-tuple-element.5), channel_id=1, source_target_pairs={{4,0},{8,4},{12,8},{16,12},{20,16},{24,20},{28,24},{32,28},{36,32}... | collective-permute-start | bytes 393224 | tf_op jit(solution)/shard_map/ppermute | solution.py:17
  22.9 0.8 copy.34
  23.6 0.7 compare_and_fusion.2
  24.3 0.1 reshape_squeeze.11
  24.5 0.0 copy-start.6
  24.5 0.0 copy-start.7
  24.5 0.0 copy-start.14
  24.6 1.2 %gather_fusion.2 = bf16[256,512]{1,0:T(8,128)(2,1)S(1)} fusion(bf16[256,512]{1,0:T(8,128)(2,1)S(1)} %all_gather.3, s32[1024]{0:T(1024)S(1)} %pad_clamp_fusion.3), kind=kCustom, calls=%fused_computation.2 | custom fusion | bytes 525312 | tf_op jit(solution)/shard_map/jit(_take)/gather | solution.py:58
  25.7 0.1 gather.31
  25.8 0.1 copy.33
  26.0 1.0 %broadcast_select_fusion = bf16[128,2,512]{2,1,0:T(2,128)(2,1)} fusion(bf16[128,2,512]{2,1,0:T(2,128)(2,1)S(1)} %gather.31, pred[128,2]{1,0:T(8,128)(4,1)S(1)} %copy.33), kind=kLoop, calls=%fused_computation.29 | loop fusion | flops 131072 | bytes 524544 | tf_op jit(solution)/shard_map/jit(_take)/select_n | solution.py:58
  27.0 15.9 %all-to-all-start = ((bf16[128,2,512]{2,1,0:T(2,128)(2,1)}), bf16[128,2,512]{2,1,0:T(2,128)(2,1)}, u32[]{:S(2)}, u32[]{:S(2)}) async-start(bf16[128,2,512]{2,1,0:T(2,128)(2,1)} %broadcast_select_fusion), calls=%async_computation | async-start | bytes 524288 | tf_op jit(solution)/shard_map/all_to_all | solution.py:61
  43.0 0.1 copy.37
  43.2 1.2 %fusion.11 = f32[64,512]{1,0:T(8,128)S(1)} fusion(bf16[1536,512]{1,0:T(8,128)(2,1)} %param.30, bf16[256,512]{1,0:T(8,128)(2,1)S(1)} %all_gather.3, s32[]{:T(128)S(6)} %select_n.82), kind=kOutput, calls=%fused_computation.26 | convolution fusion | flops 33554432 | bytes 720900 | tf_op jit(solution)/shard_map/dot_general | solution.py:68
  44.4 0.2 fusion.9
  44.7 0.1 reshape_squeeze.13
  44.9 1.0 %gather_fusion.1 = f32[256,512]{1,0:T(8,128)S(1)} fusion(f32[64,512]{1,0:T(8,128)S(1)} %fusion.11, s32[1024]{0:T(1024)S(1)} %get-tuple-element.12), kind=kCustom, calls=%fused_computation.1 | custom fusion | bytes 1049600 | tf_op jit(solution)/shard_map/jit(_take)/gather | solution.py:73
  45.8 1.5 %gather_fusion.4 = f32[128,512]{1,0:T(8,128)} fusion(f32[64,512]{1,0:T(8,128)S(1)} %fusion.11, s32[1024]{0:T(1024)S(1)} %get-tuple-element.10), kind=kCustom, calls=%fused_computation.4 | custom fusion | bytes 524800 | tf_op jit(solution)/shard_map/jit(_take)/gather | solution.py:74
  47.3 1.6 %fusion.2 = f32[512,512]{1,0:T(8,128)S(1)} fusion(bf16[128,512]{1,0:T(8,128)(2,1)} %collective-permute-done.1, bf16[256,512]{1,0:T(8,128)(2,1)S(1)} %all_gather.3, bf16[128,512]{1,0:T(8,128)(2,1)} %collective-permute-done, bf16[1536,512]{1,0:T(8,128)(2,1)} %param.30), kind=kOutput, calls=%fused_computation.16 | convolution fusion | flops 270008320 | bytes 2097152 | tf_op jit(solution)/shard_map/dot_general | solution.py:66
  48.9 1.0 %gather_fusion = f32[256,512]{1,0:T(8,128)S(1)} fusion(f32[512,512]{1,0:T(8,128)S(1)} %fusion.2, s32[1024]{0:T(1024)S(1)} %get-tuple-element.13), kind=kCustom, calls=%fused_computation | custom fusion | bytes 1049600 | tf_op jit(solution)/shard_map/jit(_take)/gather | solution.py:73
  49.9 0.1 select_add_fusion
  50.1 6.9 %all-to-all-done = bf16[128,2,512]{2,1,0:T(2,128)(2,1)} async-done(((bf16[128,2,512]{2,1,0:T(2,128)(2,1)}), bf16[128,2,512]{2,1,0:T(2,128)(2,1)}, u32[]{:S(2)}, u32[]{:S(2)}) %all-to-all-start) | async-done | bytes 262176 | tf_op jit(solution)/shard_map/all_to_all | solution.py:61
  56.9 1.1 %reshape.152 = bf16[256,512]{1,0:T(8,128)(2,1)S(1)} reshape(bf16[128,2,512]{2,1,0:T(2,128)(2,1)} %all-to-all-done) | data formatting | bytes 524288 | tf_op jit(solution)/shard_map/reshape | solution.py:61
  58.0 1.4 %fusion.15 = f32[256,512]{1,0:T(8,128)S(1)} fusion(bf16[256,512]{1,0:T(8,128)(2,1)S(1)} %reshape.152, bf16[1536,512]{1,0:T(8,128)(2,1)} %param.30), kind=kOutput, calls=%fused_computation.30 | convolution fusion | flops 134217728 | bytes 1310720 | tf_op jit(solution)/shard_map/dot_general | solution.py:67
  59.4 0.8 gather_fusion.3
  60.2 0.1 select_add_fusion.1
  60.3 1.9 %fusion.33 = (f32[384]{0:T(512)S(1)}, f32[384,512]{1,0:T(8,128)S(1)}) fusion(f32[512]{0:T(512)S(1)} %copy-done.16, bf16[512,512]{1,0:T(8,128)(2,1)S(1)} %copy-done, f32[128,512]{1,0:T(8,128)S(1)} %select_add_fusion.1, f32[256,512]{1,0:T(8,128)S(1)} %select_add_fusion, bf16[384,512]{1,0:T(8,128)(2,1)S(1)} %constant_dynamic-update-slice_fusion, ...), kind=kOutput, calls=%fused_computation.79 | convolution fusion | flops 404618880 | bytes 3020288 | tf_op jit(solution)/shard_map/dot_general | solution.py:84
  62.2 0.2 multiply_reduce_fusion
  62.5 0.2 add_convert_fusion
  62.8 0.1 copy-done.18
  62.9 1.4 %multiply_convert_fusion.1 = bf16[64,512]{1,0:T(8,128)(2,1)S(1)} fusion(f32[64,512]{1,0:T(8,128)S(1)} %fusion.9, bf16[1024,512]{1,0:T(8,128)(2,1)} %param.36, bf16[384,512]{1,0:T(8,128)(2,1)S(1)} %add_convert_fusion, f32[512]{0:T(512)S(1)} %copy-done.18, s32[384]{0:T(512)S(1)} %pad_add_fusion), kind=kOutput, calls=%fused_computation.38 | convolution fusion | flops 59006976 | bytes 1117696 | tf_op jit(solution)/shard_map/dot_general | solution.py:96
  64.4 0.3 fusion.36
  64.7 0.2 multiply_reduce_fusion.1
  64.9 0.7 copy_bitcast_fusion
  65.6 3.6 %all-to-all-start.1 = ((bf16[64,4,128]{2,0,1:T(8,128)(2,1)}), bf16[64,4,128]{2,0,1:T(8,128)(2,1)S(1)}, u32[]{:S(2)}, u32[]{:S(2)}) async-start(bf16[64,4,128]{2,0,1:T(8,128)(2,1)} %copy_bitcast_fusion), calls=%async_computation.1 | async-start | bytes 131072 | tf_op jit(solution)/shard_map/all_to_all | solution.py:104
  69.2 0.1 copy.36
  69.4 4.3 %all-to-all-done.1 = bf16[64,4,128]{2,0,1:T(8,128)(2,1)S(1)} async-done(((bf16[64,4,128]{2,0,1:T(8,128)(2,1)}), bf16[64,4,128]{2,0,1:T(8,128)(2,1)S(1)}, u32[]{:S(2)}, u32[]{:S(2)}) %all-to-all-start.1) | async-done | bytes 65568 | tf_op jit(solution)/shard_map/all_to_all | solution.py:104
  73.7 0.9 gather_fusion.5
  74.6 0.8 broadcast_select_fusion.1
  75.4 8.3 %all-to-all-start.2 = ((bf16[128,2,128]{2,1,0:T(2,128)(2,1)}), bf16[128,2,128]{2,1,0:T(2,128)(2,1)S(1)}, u32[]{:S(2)}, u32[]{:S(2)}) async-start(bf16[128,2,128]{2,1,0:T(2,128)(2,1)} %broadcast_select_fusion.1), calls=%async_computation.2 | async-start | bytes 131072 | tf_op jit(solution)/shard_map/all_to_all | solution.py:109
  83.7 0.7 slice.51
  84.4 0.7 slice.52
  85.1 10.1 %all-to-all-done.2 = bf16[128,2,128]{2,1,0:T(2,128)(2,1)S(1)} async-done(((bf16[128,2,128]{2,1,0:T(2,128)(2,1)}), bf16[128,2,128]{2,1,0:T(2,128)(2,1)S(1)}, u32[]{:S(2)}, u32[]{:S(2)}) %all-to-all-start.2) | async-done | bytes 65568 | tf_op jit(solution)/shard_map/all_to_all | solution.py:109
  95.2 0.6 copy.43
  95.8 0.6 copy.44
  (56 shorter events, 0.2 us)
Async XLA Ops:
  0.6 59.6 %copy-start = (bf16[512,512]{1,0:T(8,128)(2,1)S(1)}, bf16[512,512]{1,0:T(8,128)(2,1)}, u32[]{:S(2)}) copy-start(bf16[512,512]{1,0:T(8,128)(2,1)} %param.32) | copy-start | bytes 1572868
  11.3 36.0 %collective-permute-start = (bf16[128,512]{1,0:T(8,128)(2,1)S(1)}, bf16[128,512]{1,0:T(8,128)(2,1)}, u32[]{:S(2)}, u32[]{:S(2)}) collective-permute-start(bf16[128,512]{1,0:T(8,128)(2,1)S(1)} %get-tuple-element.4), channel_id=1, source_target_pairs={{0,4},{4,8},{8,12},{12,16},{16,20},{20,24},{24,28},{28,32},{32,36}... | collective-permute-start | bytes 393224 | tf_op jit(solution)/shard_map/ppermute | solution.py:16
  18.5 28.8 %collective-permute-start.1 = (bf16[128,512]{1,0:T(8,128)(2,1)S(1)}, bf16[128,512]{1,0:T(8,128)(2,1)}, u32[]{:S(2)}, u32[]{:S(2)}) collective-permute-start(bf16[128,512]{1,0:T(8,128)(2,1)S(1)} %get-tuple-element.5), channel_id=1, source_target_pairs={{4,0},{8,4},{12,8},{16,12},{20,16},{24,20},{28,24},{32,28},{36,32}... | collective-permute-start | bytes 393224 | tf_op jit(solution)/shard_map/ppermute | solution.py:17
  24.5 18.4 %copy-start.6 = (s32[256]{0:T(256)S(1)}, s32[256]{0:T(256)}, u32[]{:S(2)}) copy-start(s32[256]{0:T(256)} %param.25) | copy-start | bytes 3076
  24.5 18.4 %copy-start.7 = (s32[256]{0:T(256)S(1)}, s32[256]{0:T(256)}, u32[]{:S(2)}) copy-start(s32[256]{0:T(256)} %param.24) | copy-start | bytes 3076
  24.5 18.4 %copy-start.13 = (s32[128]{0:T(128)S(1)}, s32[128]{0:T(128)}, u32[]{:S(2)}) copy-start(s32[128]{0:T(128)} %param.27) | copy-start | bytes 1540
  24.5 18.4 %copy-start.15 = (s32[128]{0:T(128)S(1)}, s32[128]{0:T(128)}, u32[]{:S(2)}) copy-start(s32[128]{0:T(128)} %param.26) | copy-start | bytes 1540
  24.5 18.5 %copy-start.14 = (s32[1,128,2]{1,2,0:T(2,128)S(1)}, s32[1,128,2]{1,2,0:T(2,128)}, u32[]{:S(2)}) copy-start(s32[1,128,2]{1,2,0:T(2,128)} %param.29) | copy-start | bytes 3076
  24.5 18.6 %copy-start.4 = (bf16[256,512]{1,0:T(8,128)(2,1)S(1)}, bf16[256,512]{1,0:T(8,128)(2,1)}, u32[]{:S(2)}) copy-start(bf16[256,512]{1,0:T(8,128)(2,1)} %param.22) | copy-start | bytes 786436
  25.7 18.7 %copy-start.3 = (bf16[1024,512]{1,0:T(8,128)(2,1)S(1)}, bf16[1024,512]{1,0:T(8,128)(2,1)}, u32[]{:S(2)}) copy-start(bf16[1024,512]{1,0:T(8,128)(2,1)} %param.36) | copy-start | bytes 3145732
  27.0 29.9 %all-to-all-start = ((bf16[128,2,512]{2,1,0:T(2,128)(2,1)}), bf16[128,2,512]{2,1,0:T(2,128)(2,1)}, u32[]{:S(2)}, u32[]{:S(2)}) async-start(bf16[128,2,512]{2,1,0:T(2,128)(2,1)} %broadcast_select_fusion), calls=%async_computation | async-start | bytes 524288 | tf_op jit(solution)/shard_map/all_to_all | solution.py:61
  45.8 1.5 %copy-start.5 = (bf16[128,512]{1,0:T(8,128)(2,1)S(1)}, bf16[128,512]{1,0:T(8,128)(2,1)}, u32[]{:S(2)}) copy-start(bf16[128,512]{1,0:T(8,128)(2,1)} %param.23) | copy-start | bytes 393220
  58.0 2.2 %copy-start.1 = (f32[128,512]{1,0:T(8,128)S(1)}, f32[128,512]{1,0:T(8,128)}, u32[]{:S(2)}) copy-start(f32[128,512]{1,0:T(8,128)} %gather_fusion.4) | copy-start | bytes 786436
  59.4 0.9 copy-start.16
  59.4 0.9 copy-start.17
  60.3 2.2 %copy-start.8 = (f32[512]{0:T(512)S(1)}, f32[512]{0:T(512)}, u32[]{:S(2)}) copy-start(f32[512]{0:T(512)} %param.35) | copy-start | bytes 6148
  60.3 2.2 %copy-start.9 = (f32[512]{0:T(512)S(1)}, f32[512]{0:T(512)}, u32[]{:S(2)}) copy-start(f32[512]{0:T(512)} %param.34) | copy-start | bytes 6148
  62.2 0.7 copy-start.18
  62.5 1.9 %copy-start.2 = (bf16[512,512]{1,0:T(8,128)(2,1)S(1)}, bf16[512,512]{1,0:T(8,128)(2,1)}, u32[]{:S(2)}) copy-start(bf16[512,512]{1,0:T(8,128)(2,1)} %param.38) | copy-start | bytes 1572868
  62.5 1.9 %copy-start.10 = (f32[512]{0:T(512)S(1)}, f32[512]{0:T(512)}, u32[]{:S(2)}) copy-start(f32[512]{0:T(512)} %param.39) | copy-start | bytes 6148
  62.9 2.0 %copy-start.11 = (f32[512]{0:T(512)S(1)}, f32[512]{0:T(512)}, u32[]{:S(2)}) copy-start(f32[512]{0:T(512)} %param.41) | copy-start | bytes 6148
  62.9 2.0 %copy-start.12 = (f32[512]{0:T(512)S(1)}, f32[512]{0:T(512)}, u32[]{:S(2)}) copy-start(f32[512]{0:T(512)} %param.40) | copy-start | bytes 6148
  65.6 8.1 %all-to-all-start.1 = ((bf16[64,4,128]{2,0,1:T(8,128)(2,1)}), bf16[64,4,128]{2,0,1:T(8,128)(2,1)S(1)}, u32[]{:S(2)}, u32[]{:S(2)}) async-start(bf16[64,4,128]{2,0,1:T(8,128)(2,1)} %copy_bitcast_fusion), calls=%async_computation.1 | async-start | bytes 131072 | tf_op jit(solution)/shard_map/all_to_all | solution.py:104
  75.4 19.8 %all-to-all-start.2 = ((bf16[128,2,128]{2,1,0:T(2,128)(2,1)}), bf16[128,2,128]{2,1,0:T(2,128)(2,1)S(1)}, u32[]{:S(2)}, u32[]{:S(2)}) async-start(bf16[128,2,128]{2,1,0:T(2,128)(2,1)} %broadcast_select_fusion.1), calls=%async_computation.2 | async-start | bytes 131072 | tf_op jit(solution)/shard_map/all_to_all | solution.py:109
where the time goes:
time: 97 us; the launch traced here: 96.4 us
  starting transfers between devices  39.3 us (41%)
  waiting for transfers between devices  21.3 us (22%)
  local copies, waits for them, and re-layouts  11.7 us (12%)
  blocking collectives  10.6 us (11%)
  matrix products  8.07 us (8%)
  other arithmetic  4.32 us (4%)
  between operations  1.18 us (1%)
    all_to_all x1, starting transfers between devices, body(): lax.all_to_all(outgoing, 'patch', split_axis=0, concat_axis=0, tiled=True)  15.9 us
    all_gather x1, blocking collectives, body(): full_rows = lax.all_gather(nodes, 'lat', axis=1, tiled=True)  10.6 us
    all_to_all x1, waiting for transfers between devices, body(): lax.all_to_all(tile_send, 'patch', split_axis=0, concat_axis=0, tiled=True)  10.1 us
    all_to_all x1, starting transfers between devices, body(): lax.all_to_all(tile_send, 'patch', split_axis=0, concat_axis=0, tiled=True)  8.31 us
    ppermute x1, starting transfers between devices, with_halo(): before = lax.ppermute(last, axis, up)  7.17 us
    all_to_all x1, waiting for transfers between devices, body(): lax.all_to_all(outgoing, 'patch', split_axis=0, concat_axis=0, tiled=True)  6.85 us
    ppermute x1, starting transfers between devices, with_halo(): after = lax.ppermute(initial, axis, down)  4.37 us
    all_to_all x1, waiting for transfers between devices, body(): lax.all_to_all(updated_own, 'lat', split_axis=1, concat_axis=0, tiled=True)  4.33 us
  transfers between devices with their start and end apart: 5, of which 3 were waited for; matrix products, arithmetic and copies ran while one was open for 13% of the time, Pallas kernels for 0%

commit v1 on v0

v1 whole, which is shorter than its diff:
```python
import functools

import jax
import jax.numpy as jnp
from jax import lax
from jax.experimental import pallas as pl
from jax.experimental.pallas import tpu as pltpu
from jax.sharding import PartitionSpec as P

HALO = 128
LANES = 128
F32 = jnp.float32
BF16 = jnp.bfloat16


def matmul(a, b):
    return jnp.dot(a, b, preferred_element_type=F32)


def silu(v):
    return v / (1.0 + jnp.exp(-v))


def norm_rows(values, gain_row, shift_row):
    average = jnp.mean(values, axis=-1, keepdims=True)
    centered = values - average
    variance = jnp.mean(centered * centered, axis=-1, keepdims=True)
    return centered * lax.rsqrt(variance + 1e-05) * gain_row + shift_row


def column(row):
    shape = (LANES, LANES)
    same = lax.broadcasted_iota(jnp.int32, shape, 0) == lax.broadcasted_iota(jnp.int32, shape, 1)
    return jnp.sum(jnp.where(same, row.astype(F32), 0.0), axis=1, keepdims=True)


def columns(rows):
    return jnp.concatenate([column(rows[i : i + 1]) for i in range(rows.shape[0])], axis=0)


def pick(index_column, count):
    shape = (index_column.shape[0], count)
    places = lax.broadcasted_iota(jnp.int32, shape, 1).astype(F32)
    return jnp.where(places == index_column, 1.0, 0.0).astype(BF16)


def spread(index_rows, repeat):
    shape = (LANES * repeat, LANES)
    line = lax.broadcasted_iota(jnp.int32, shape, 0)
    patch = lax.broadcasted_iota(jnp.int32, shape, 1)
    here = lax.div(line, repeat) == patch
    odd = lax.rem(line, 2) == 1
    values = jnp.where(odd, index_rows[1:2].astype(F32), index_rows[0:1].astype(F32))
    return jnp.sum(jnp.where(here, values, 0.0), axis=1, keepdims=True)


def far_kernel(full_ref, rows_ref, out_ref, coarse, *, coarse_rows):
    chunks = full_ref.shape[0]
    per = 2 * chunks
    for c in range(chunks):
        coarse[c * coarse_rows : (c + 1) * coarse_rows, :] = full_ref[c, :coarse_rows, :]
    line = lax.broadcasted_iota(jnp.int32, (LANES * per, 1), 0)
    chunk = lax.div(lax.rem(line, per), 2)
    place = spread(rows_ref[...], per) + (chunk * coarse_rows).astype(F32)
    out_ref[...] = matmul(pick(place, chunks * coarse_rows), coarse[...]).astype(BF16)


def short_kernel(
    full_ref,
    before_ref,
    after_ref,
    short_ref,
    long_ref,
    send_ref,
    short_recv_ref,
    long_recv_ref,
    w_in_ref,
    b_in_ref,
    w_out_ref,
    b_out_ref,
    gain_ref,
    shift_ref,
    node_w_ref,
    node_b_ref,
    short_new_ref,
    long_pre_ref,
    sum_ref,
    node_pre_ref,
    own_ref,
    halo,
):
    chunks, rows, width = full_ref.shape
    quarter = own_ref.shape[0]
    latent = chunks * width
    start = pl.multiple_of(lax.axis_index("lat") * quarter, quarter)
    for c in range(chunks):
        lanes = slice(c * width, (c + 1) * width)
        halo[:HALO, lanes] = before_ref[c]
        halo[HALO : HALO + rows, lanes] = full_ref[c]
        halo[HALO + rows :, lanes] = after_ref[c]
        own_ref[:, lanes] = full_ref[c, pl.ds(start, quarter), :]
    own = own_ref[...]
    w_self = w_in_ref[:latent, :]
    w_send = w_in_ref[latent : 2 * latent, :]
    w_recv = w_in_ref[2 * latent :, :]
    recv_short = matmul(pick(columns(short_recv_ref[...]), quarter), own).astype(BF16)
    recv_long = matmul(pick(columns(long_recv_ref[...]), quarter), own).astype(BF16)
    sent = matmul(pick(columns(send_ref[...]), halo.shape[0]), halo[...]).astype(BF16)
    edges = short_ref[...]
    pre = matmul(edges, w_self) + matmul(sent, w_send) + matmul(recv_short, w_recv) + b_in_ref[...]
    hidden = silu(pre).astype(BF16)
    output = matmul(hidden, w_out_ref[...]) + b_out_ref[...]
    updated = (edges.astype(F32) + norm_rows(output, gain_ref[...], shift_ref[...])).astype(BF16)
    short_new_ref[...] = updated
    receivers = short_recv_ref[...]
    total = jnp.zeros((quarter, latent), F32)
    for i in range(receivers.shape[0]):
        mine = lax.broadcasted_iota(jnp.int32, (quarter, LANES), 0) == receivers[i : i + 1]
        hot = jnp.where(mine, 1.0, 0.0).astype(BF16)
        total = total + matmul(hot, updated[i * LANES : (i + 1) * LANES])
    sum_ref[...] = total
    long_pre_ref[...] = matmul(long_ref[...], w_self) + matmul(recv_long, w_recv) + b_in_ref[...]
    node_pre_ref[...] = matmul(own, node_w_ref[:latent, :]) + node_b_ref[...]


def long_kernel(
    far_ref,
    long_ref,
    long_pre_ref,
    sum_ref,
    node_pre_ref,
    own_ref,
    send_ref,
    recv_ref,
    w_in_ref,
    w_out_ref,
    b_out_ref,
    gain_ref,
    shift_ref,
    node_w_ref,
    node_w_out_ref,
    node_b_out_ref,
    node_gain_ref,
    node_shift_ref,
    long_new_ref,
    own_new_ref,
):
    chunks, quarter, width = own_new_ref.shape
    latent = chunks * width
    per = 2 * chunks
    send = columns(send_ref[...])
    source = jnp.floor(send * 0.5)
    place = source * per + (send - 2.0 * source)
    far = far_ref[...]
    pre = long_pre_ref[...]
    for c in range(chunks):
        sent = matmul(pick(place + 2.0 * c, far.shape[0]), far).astype(BF16)
        first = latent + c * width
        pre = pre + matmul(sent, w_in_ref[first : first + width, :])
    hidden = silu(pre).astype(BF16)
    output = matmul(hidden, w_out_ref[...]) + b_out_ref[...]
    updated = (long_ref[...].astype(F32) + norm_rows(output, gain_ref[...], shift_ref[...])).astype(BF16)
    long_new_ref[...] = updated
    mine = lax.broadcasted_iota(jnp.int32, (quarter, LANES), 0) == recv_ref[...]
    hot = jnp.where(mine, 1.0, 0.0).astype(BF16)
    aggregate = (sum_ref[...] + matmul(hot, updated)).astype(BF16)
    node_pre = node_pre_ref[...] + matmul(aggregate, node_w_ref[latent:, :])
    node_hidden = silu(node_pre).astype(BF16)
    node_out = matmul(node_hidden, node_w_out_ref[...]) + node_b_out_ref[...]
    new = own_ref[...].astype(F32) + norm_rows(node_out, node_gain_ref[...], node_shift_ref[...])
    new = new.astype(BF16)
    for c in range(chunks):
        own_new_ref[c] = new[:, c * width : (c + 1) * width]


def tile_kernel(rows_ref, index_ref, out_ref):
    out_ref[...] = matmul(pick(spread(index_ref[...], 2), rows_ref.shape[0]), rows_ref[...]).astype(BF16)


def call(kernel, outs, operands, flops, scratch=()):
    moved = sum(x.size * x.dtype.itemsize for x in (*operands, *outs))
    return pl.pallas_call(
        kernel,
        out_shape=tuple(outs),
        in_specs=[pl.BlockSpec(memory_space=pltpu.VMEM)] * len(operands),
        out_specs=tuple(pl.BlockSpec(memory_space=pltpu.VMEM) for _ in outs),
        scratch_shapes=list(scratch),
        compiler_params=pltpu.CompilerParams(vmem_limit_bytes=24 * 1024 * 1024),
        cost_estimate=pl.CostEstimate(flops=flops, bytes_accessed=moved, transcendentals=0),
    )(*operands)


def shape(dims, dtype=BF16):
    return jax.ShapeDtypeStruct(dims, dtype)


def body(
    nodes,
    short_edges,
    long_edges,
    short_send,
    short_recv,
    long_send,
    long_recv,
    send_rows,
    tile_rows,
    edge_w_in,
    edge_b_in,
    edge_w_out,
    edge_b_out,
    edge_gain,
    edge_shift,
    node_w_in,
    node_b_in,
    node_w_out,
    node_b_out,
    node_gain,
    node_shift,
):
    latent = edge_w_out.shape[0]
    rows, width = nodes.shape
    patches, lats = lax.axis_size("patch"), lax.axis_size("lat")
    quarter = rows // lats
    shorts, longs = short_edges.shape[0], long_edges.shape[0]
    row = lambda v: v.reshape(1, latent)

    copies = jnp.broadcast_to(nodes[None], (lats, rows, width))
    full = lax.all_to_all(copies, "lat", split_axis=0, concat_axis=0, tiled=True)

    (outgoing,) = call(
        functools.partial(far_kernel, coarse_rows=16),
        [shape((patches * 2 * lats, width))],
        [full, send_rows[0].T],
        2 * patches * 2 * lats * 64 * width,
        [pltpu.VMEM((lats * 16, width), BF16)],
    )
    outgoing = outgoing.reshape(patches, 2 * lats, width)
    arrived = lax.all_to_all(outgoing, "patch", split_axis=0, concat_axis=0, tiled=True)

    up = [(i, (i + 1) % patches) for i in range(patches)]
    down = [(j, i) for i, j in up]
    before = lax.ppermute(full[:, rows - HALO :], "patch", up)
    after = lax.ppermute(full[:, :HALO], "patch", down)
    short_new, long_pre, total, node_pre, own = call(
        short_kernel,
        [
            shape((shorts, latent)),
            shape((longs, latent), F32),
            shape((quarter, latent), F32),
            shape((quarter, latent), F32),
            shape((quarter, latent)),
        ],
        [
            full,
            before,
            after,
            short_edges,
            long_edges,
            short_send.reshape(-1, LANES),
            short_recv.reshape(-1, LANES),
            long_recv.reshape(-1, LANES),
            edge_w_in,
            row(edge_b_in),
            edge_w_out,
            row(edge_b_out),
            row(edge_gain),
            row(edge_shift),
            node_w_in,
            row(node_b_in),
        ],
        2 * 400 * 512 * 512 * 4,
        [pltpu.VMEM((rows + 2 * HALO, latent), BF16)],
    )
    long_new, own_new = call(
        long_kernel,
        [shape((longs, latent)), shape((lats, quarter, width))],
        [
            arrived.reshape(patches * 2 * lats, width),
            long_edges,
            long_pre,
            total,
            node_pre,
            own,
            long_send.reshape(-1, LANES),
            long_recv.reshape(-1, LANES),
            edge_w_in,
            edge_w_out,
            row(edge_b_out),
            row(edge_gain),
            row(edge_shift),
            node_w_in,
            node_w_out,
            row(node_b_out),
            row(node_gain),
            row(node_shift),
        ],
        2 * 200 * 512 * 512 * 4,
    )
    node_rows = lax.all_to_all(own_new, "lat", split_axis=0, concat_axis=0, tiled=True).reshape(rows, width)
    (tile_send,) = call(
        tile_kernel,
        [shape((patches * 2, width))],
        [node_rows, tile_rows[0].T],
        2 * patches * 2 * rows * width,
    )
    tiles = lax.all_to_all(
        tile_send.reshape(patches, 2, width), "patch", split_axis=0, concat_axis=0, tiled=True
    ).reshape(patches * 2, width)
    return (short_new, long_new, node_rows, tiles)


def solution(mesh):
    placed = (
        P("patch", "lat"),
        P(("patch", "lat"), None),
        P(("patch", "lat"), None),
        P(("patch", "lat")),
        P(("patch", "lat")),
        P(("patch", "lat")),
        P(("patch", "lat")),
        P("patch", None, None),
        P("patch", None, None),
    ) + (P(),) * 12
    return jax.shard_map(
        body,
        mesh=mesh,
        in_specs=placed,
        out_specs=(
            P(("patch", "lat"), None),
            P(("patch", "lat"), None),
            P("patch", "lat"),
            P("patch", "lat"),
        ),
        check_vma=False,
    )
```

time: 97 us -> 99.4 us (1.025)
  blocking collectives: 10.6 us -> 40.8 us
  waiting for transfers between devices: 21.3 us -> 6.18 us
  starting transfers between devices: 39.3 us -> 24.9 us
  matrix products: 8.07 us -> 0 us
  Pallas kernels: 0 us -> 7.42 us
  local copies, waits for them, and re-layouts: 11.7 us -> 18.5 us
  other arithmetic: 4.32 us -> 0 us
    all_to_all x0 -> x3, blocking collectives: none -> 40.8 us  [the longest x1 23.8 us: body(): lax.all_to_all(tile_send.reshape(patches, 2, width), 'patch', split_axis=...]
    unnamed x43 -> x62, local copies, waits for them, and re-layouts: 2.41 us -> 17.5 us
    all_to_all x2 -> x0, waiting for transfers between devices: 14.4 us -> none  [the longest x1 10.1 us: body(): lax.all_to_all(tile_send, 'patch', split_axis=0, concat_axis=0, tiled=True)]
    all_to_all x2 -> x0, starting transfers between devices: 11.9 us -> none  [the longest x1 8.31 us: body(): lax.all_to_all(tile_send, 'patch', split_axis=0, concat_axis=0, tiled=True)]
    all_gather x1 -> x0, blocking collectives: 10.6 us -> none  [body(): full_rows = lax.all_gather(nodes, 'lat', axis=1, tiled=True)]
    dot_general x7 -> x0, matrix products: 8.07 us -> none  [the longest x1 1.87 us: body(): jnp.dot(hidden, edge_w_out, preferred_element_type=jnp.float32) + edge_b_out]
    pallas_call x0 -> x4, Pallas kernels: none -> 7.42 us  [call(): pl.pallas_call(kernel, out_shape=tuple(outs), in_specs=[pl.BlockSpec(memo...]
    all_to_all x1, waiting for transfers between devices: 6.85 us -> 0.01 us  [body(): lax.all_to_all(outgoing, 'patch', split_axis=0, concat_axis=0, tiled=True)]
  transfers between devices with their start and end apart: 5 -> 3, of which waited for: 3 -> 2; matrix products, arithmetic and copies ran while one was open for 13% -> 0% of each run, Pallas kernels for 0% -> 3%
where the time goes in v1:
time: 99.4 us; the launch traced here: 98.7 us
  blocking collectives  40.8 us (41%)
  starting transfers between devices  24.9 us (25%)
  local copies, waits for them, and re-layouts  18.5 us (19%)
  Pallas kernels  7.42 us (7%)
  waiting for transfers between devices  6.18 us (6%)
    all_to_all x1, blocking collectives, body(): lax.all_to_all(tile_send.reshape(patches, 2, width), 'patch', split_axis=...  23.8 us
    all_to_all x1, starting transfers between devices, body(): lax.all_to_all(outgoing, 'patch', split_axis=0, concat_axis=0, tiled=True)  19.5 us
    unnamed x62, local copies, waits for them, and re-layouts  17.5 us
    all_to_all x1, blocking collectives, body(): lax.all_to_all(copies, 'lat', split_axis=0, concat_axis=0, tiled=True)  10.2 us
    pallas_call x4, Pallas kernels, call(): pl.pallas_call(kernel, out_shape=tuple(outs), in_specs=[pl.BlockSpec(memo...  7.42 us
    all_to_all x1, blocking collectives, body(): lax.all_to_all(own_new, 'lat', split_axis=0, concat_axis=0, tiled=True)  6.83 us
    ppermute x1, starting transfers between devices, body(): before = lax.ppermute(full[:, rows - HALO:], 'patch', up)  3.54 us
    ppermute x1, waiting for transfers between devices, body(): after = lax.ppermute(full[:, :HALO], 'patch', down)  3.14 us
  transfers between devices with their start and end apart: 3, of which 2 were waited for; matrix products, arithmetic and copies ran while one was open for 0% of the time, Pallas kernels for 3%

profile of v1, /device:TPU:1, one launch (start us, length us, event | category | flops | bytes accessed | tf_op | source)
XLA Modules:
  0.0 98.7 jit_solution(10973461702314813157)
XLA Ops:
  0.6 0.0 copy-start.15
  0.6 0.0 copy-start.16
  0.7 0.0 copy-start.17
  0.7 0.0 copy-start.18
  0.7 0.0 copy-start.5
  0.7 0.0 copy-start
  0.7 1.0 %broadcast_in_dim.2 = bf16[4,256,128]{2,1,0:T(8,128)(2,1)S(1)} broadcast(bf16[256,128]{1,0:T(8,128)(2,1)} %param.21), dimensions={1,2} | broadcast | bytes 327680 | tf_op jit(solution)/shard_map/broadcast_in_dim | solution.py:227
  1.7 10.2 %all_to_all.20.full_ref = bf16[4,256,128]{2,1,0:T(8,128)(2,1)S(1)} all-to-all(bf16[4,256,128]{2,1,0:T(8,128)(2,1)S(1)} %broadcast_in_dim.2), channel_id=1, replica_groups=mesh['patch'=128,'lat'=4] {'lat'}, dimensions={0} | all-to-all | bytes 524288 | tf_op jit(solution)/shard_map/all_to_all | solution.py:228
  11.9 0.7 copy-done.25
  12.6 1.1 %shard_map.229 = bf16[1024,128]{1,0:T(8,128)(2,1)} custom-call(bf16[4,256,128]{2,1,0:T(8,128)(2,1)S(1)} %all_to_all.20.full_ref, s32[2,128]{1,0:T(2,128)S(1)} %bitcast.39), custom_call_target="tpu_custom_call" | custom-call | flops 16777216 | bytes 525312 | tf_op jit(solution)/shard_map/pallas_call | solution.py:182
  13.7 19.5 %all-to-all-start.1 = ((bf16[128,8,128]{2,1,0:T(8,128)(2,1)}), bf16[128,8,128]{2,1,0:T(8,128)(2,1)}, u32[]{:S(2)}, u32[]{:S(2)}) async-start(bf16[128,8,128]{2,1,0:T(8,128)(2,1)} %bitcast.10), calls=%async_computation.1 | async-start | bytes 524288 | tf_op jit(solution)/shard_map/all_to_all | solution.py:238
  33.2 3.5 %collective-permute-start = (bf16[4,128,128]{2,1,0:T(8,128)(2,1)S(1)}, bf16[4,128,128]{2,1,0:T(8,128)(2,1)S(1)}, u32[]{:S(2)}, u32[]{:S(2)}) collective-permute-start(bf16[4,128,128]{2,1,0:T(8,128)(2,1)S(1)} %get-tuple-element.19), channel_id=1, source_target_pairs={{0,4},{4,8},{8,12},{12,16},{16,20},{20,24},{24,28},{28,32},{32,36}... | collective-permute-start | bytes 393224 | tf_op jit(solution)/shard_map/ppermute | solution.py:242
  36.7 1.9 %collective-permute-start.1 = (bf16[4,128,128]{2,1,0:T(8,128)(2,1)S(1)}, bf16[4,128,128]{2,1,0:T(8,128)(2,1)S(1)}, u32[]{:S(2)}, u32[]{:S(2)}) collective-permute-start(bf16[4,128,128]{2,1,0:T(8,128)(2,1)S(1)} %get-tuple-element.18), channel_id=1, source_target_pairs={{4,0},{8,4},{12,8},{16,12},{20,16},{24,20},{28,24},{32,28},{36,32}... | collective-permute-start | bytes 393224 | tf_op jit(solution)/shard_map/ppermute | solution.py:243
  38.7 3.0 %collective-permute-done.before_ref = bf16[4,128,128]{2,1,0:T(8,128)(2,1)S(1)} collective-permute-done((bf16[4,128,128]{2,1,0:T(8,128)(2,1)S(1)}, bf16[4,128,128]{2,1,0:T(8,128)(2,1)S(1)}, u32[]{:S(2)}, u32[]{:S(2)}) %collective-permute-start) | collective-permute-done | bytes 131104 | tf_op jit(solution)/shard_map/ppermute | solution.py:242
  41.7 3.1 %collective-permute-done.1.after_ref = bf16[4,128,128]{2,1,0:T(8,128)(2,1)S(1)} collective-permute-done((bf16[4,128,128]{2,1,0:T(8,128)(2,1)S(1)}, bf16[4,128,128]{2,1,0:T(8,128)(2,1)S(1)}, u32[]{:S(2)}, u32[]{:S(2)}) %collective-permute-start.1) | collective-permute-done | bytes 131104 | tf_op jit(solution)/shard_map/ppermute | solution.py:243
  44.9 0.0 copy-done.18
  44.9 0.0 copy-done.5
  44.9 0.0 copy-done
  44.9 0.0 copy-done.3
  44.9 0.0 copy-start.1
  44.9 1.2 %copy-done.1 = bf16[1024,512]{1,0:T(8,128)(2,1)S(1)} copy-done((bf16[1024,512]{1,0:T(8,128)(2,1)S(1)}, bf16[1024,512]{1,0:T(8,128)(2,1)}, u32[]{:S(2)}) %copy-start.1) | copy-done | bytes 1048600
  46.1 0.9 copy-done.6
  47.1 0.7 copy-done.19
  47.8 0.7 copy-done.23
  48.4 0.7 copy-done.26
  49.1 0.7 copy-done.27
  49.8 2.6 %shard_map.228 = (bf16[256,512]{1,0:T(8,128)(2,1)}, f32[128,512]{1,0:T(8,128)S(1)}, f32[64,512]{1,0:T(8,128)S(1)}, f32[64,512]{1,0:T(8,128)S(1)}, bf16[64,512]{1,0:T(8,128)(2,1)S(1)}) custom-call(bf16[4,256,128]{2,1,0:T(8,128)(2,1)S(1)} %all_to_all.20.full_ref, bf16[4,128,128]{2,1,0:T(8,128)(2,1)S(1)} %collective-permute-done.before_ref, ...), custom_call_target="tpu_custom_call" | custom-call | flops 838860800 | bytes 4928000 | tf_op jit(solution)/shard_map/pallas_call | solution.py:182
  52.4 0.7 copy-done.7
  53.1 0.7 copy-done.9
  53.8 0.7 copy-done.11
  54.4 0.6 copy-done.13
  55.1 0.0 all-to-all-done.1
  55.1 1.0 %copy-done.4 = bf16[512,512]{1,0:T(8,128)(2,1)S(1)} copy-done((bf16[512,512]{1,0:T(8,128)(2,1)S(1)}, bf16[512,512]{1,0:T(8,128)(2,1)}, u32[]{:S(2)}) %copy-start.4) | copy-done | bytes 524312
  56.1 0.9 copy-done.8
  57.1 0.9 copy-done.10
  58.0 0.9 copy-done.12
  58.9 0.8 copy-done.14
  59.7 0.7 copy-done.20
  60.4 0.7 copy-done.21
  61.1 0.7 copy-done.22
  61.7 0.7 copy-done.24
  62.4 0.7 copy-done.29
  63.1 3.4 %shard_map.230 = (bf16[128,512]{1,0:T(8,128)(2,1)}, bf16[4,64,128]{2,1,0:T(8,128)(2,1)S(1)}) custom-call(bf16[1024,128]{1,0:T(8,128)(2,1)} %bitcast.11.far_ref, bf16[128,512]{1,0:T(8,128)(2,1)S(1)} %copy-done.5, f32[128,512]{1,0:T(8,128)S(1)} %copy-done.8, f32[64,512]{1,0:T(8,128)S(1)} %copy-done.10, f32[64,512]{1,0:T(8,128)S(1)} %copy-done.12, ...), custom_call_target="tpu_custom_call" | custom-call | flops 419430400 | bytes 4862976 | tf_op jit(solution)/shard_map/pallas_call | solution.py:182
  66.5 6.8 %all_to_all.21 = bf16[4,64,128]{2,1,0:T(8,128)(2,1)S(1)} all-to-all(bf16[4,64,128]{2,1,0:T(8,128)(2,1)S(1)} %get-tuple-element.17), channel_id=1, replica_groups=mesh['patch'=128,'lat'=4] {'lat'}, dimensions={0} | all-to-all | bytes 131072 | tf_op jit(solution)/shard_map/all_to_all | solution.py:299
  73.3 0.2 shard_map.231
  73.6 23.8 %all_to_all.22 = bf16[128,2,128]{2,1,0:T(2,128)(2,1)S(1)} all-to-all(bf16[128,2,128]{2,1,0:T(2,128)(2,1)S(1)} %bitcast.25), channel_id=1, replica_groups=mesh['patch'=128,'lat'=4] {'patch'}, dimensions={0} | all-to-all | bytes 131072 | tf_op jit(solution)/shard_map/all_to_all | solution.py:306
  97.4 0.6 copy.27
  98.0 0.6 copy.28
  (29 shorter events, 0.1 us)
Async XLA Ops:
  0.6 44.2 %copy-start.15 = (f32[512]{0:T(512)S(1)}, f32[512]{0:T(512)}, u32[]{:S(2)}) copy-start(f32[512]{0:T(512)} %param.33) | copy-start | bytes 6148
  0.6 44.2 %copy-start.16 = (f32[512]{0:T(512)S(1)}, f32[512]{0:T(512)}, u32[]{:S(2)}) copy-start(f32[512]{0:T(512)} %param.34) | copy-start | bytes 6148
  0.7 44.2 %copy-start.17 = (f32[512]{0:T(512)S(1)}, f32[512]{0:T(512)}, u32[]{:S(2)}) copy-start(f32[512]{0:T(512)} %param.35) | copy-start | bytes 6148
  0.7 44.2 %copy-start.18 = (f32[512]{0:T(512)S(1)}, f32[512]{0:T(512)}, u32[]{:S(2)}) copy-start(f32[512]{0:T(512)} %param.31) | copy-start | bytes 6148
  0.7 44.2 %copy-start.5 = (bf16[128,512]{1,0:T(8,128)(2,1)S(1)}, bf16[128,512]{1,0:T(8,128)(2,1)}, u32[]{:S(2)}) copy-start(bf16[128,512]{1,0:T(8,128)(2,1)} %long_ref.3) | copy-start | bytes 393220
  0.7 44.2 %copy-start = (bf16[1536,512]{1,0:T(8,128)(2,1)S(1)}, bf16[1536,512]{1,0:T(8,128)(2,1)}, u32[]{:S(2)}) copy-start(bf16[1536,512]{1,0:T(8,128)(2,1)} %w_in_ref.3) | copy-start | bytes 4718596
  0.7 44.2 %copy-start.3 = (bf16[512,512]{1,0:T(8,128)(2,1)S(1)}, bf16[512,512]{1,0:T(8,128)(2,1)}, u32[]{:S(2)}) copy-start(bf16[512,512]{1,0:T(8,128)(2,1)} %w_out_ref.3) | copy-start | bytes 1572868
  11.9 0.7 copy-start.25
  13.7 41.4 %all-to-all-start.1 = ((bf16[128,8,128]{2,1,0:T(8,128)(2,1)}), bf16[128,8,128]{2,1,0:T(8,128)(2,1)}, u32[]{:S(2)}, u32[]{:S(2)}) async-start(bf16[128,8,128]{2,1,0:T(8,128)(2,1)} %bitcast.10), calls=%async_computation.1 | async-start | bytes 524288 | tf_op jit(solution)/shard_map/all_to_all | solution.py:238
  33.2 8.5 %collective-permute-start = (bf16[4,128,128]{2,1,0:T(8,128)(2,1)S(1)}, bf16[4,128,128]{2,1,0:T(8,128)(2,1)S(1)}, u32[]{:S(2)}, u32[]{:S(2)}) collective-permute-start(bf16[4,128,128]{2,1,0:T(8,128)(2,1)S(1)} %get-tuple-element.19), channel_id=1, source_target_pairs={{0,4},{4,8},{8,12},{12,16},{16,20},{20,24},{24,28},{28,32},{32,36}... | collective-permute-start | bytes 393224 | tf_op jit(solution)/shard_map/ppermute | solution.py:242
  36.7 8.1 %collective-permute-start.1 = (bf16[4,128,128]{2,1,0:T(8,128)(2,1)S(1)}, bf16[4,128,128]{2,1,0:T(8,128)(2,1)S(1)}, u32[]{:S(2)}, u32[]{:S(2)}) collective-permute-start(bf16[4,128,128]{2,1,0:T(8,128)(2,1)S(1)} %get-tuple-element.18), channel_id=1, source_target_pairs={{4,0},{8,4},{12,8},{16,12},{20,16},{24,20},{28,24},{32,28},{36,32}... | collective-permute-start | bytes 393224 | tf_op jit(solution)/shard_map/ppermute | solution.py:243
  44.9 1.2 %copy-start.1 = (bf16[1024,512]{1,0:T(8,128)(2,1)S(1)}, bf16[1024,512]{1,0:T(8,128)(2,1)}, u32[]{:S(2)}) copy-start(bf16[1024,512]{1,0:T(8,128)(2,1)} %node_w_ref.3) | copy-start | bytes 3145732
  46.1 0.9 copy-start.6
  47.1 0.7 copy-start.19
  47.8 0.7 copy-start.23
  48.4 0.7 copy-start.26
  49.1 0.7 copy-start.27
  49.8 5.3 %copy-start.2 = (bf16[1024,512]{1,0:T(8,128)(2,1)S(1)}, bf16[1024,512]{1,0:T(8,128)(2,1)}, u32[]{:S(2)}) copy-start(bf16[1024,512]{1,0:T(8,128)(2,1)} %node_w_ref.3) | copy-start | bytes 3145732
  52.4 0.7 copy-start.7
  53.1 0.7 copy-start.9
  53.8 0.7 copy-start.11
  54.4 0.6 copy-start.13
  55.1 1.0 %copy-start.4 = (bf16[512,512]{1,0:T(8,128)(2,1)S(1)}, bf16[512,512]{1,0:T(8,128)(2,1)}, u32[]{:S(2)}) copy-start(bf16[512,512]{1,0:T(8,128)(2,1)} %node_w_out_ref.1) | copy-start | bytes 1572868
  56.1 0.9 copy-start.8
  57.1 0.9 copy-start.10
  58.0 0.9 copy-start.12
  58.9 0.8 copy-start.14
  59.7 0.7 copy-start.20
  60.4 0.7 copy-start.21
  61.1 0.7 copy-start.22
  61.7 0.7 copy-start.24
  62.4 0.7 copy-start.29
  63.1 10.3 %copy-start.28 = (s32[1,128,2]{1,2,0:T(2,128)S(1)}, s32[1,128,2]{1,2,0:T(2,128)}, u32[]{:S(2)}) copy-start(s32[1,128,2]{1,2,0:T(2,128)} %param.29) | copy-start | bytes 3076

commit v2 on v0

v2 whole, which is shorter than its diff:
```python
import functools

import jax
import jax.numpy as jnp
from jax import lax
from jax.experimental import pallas as pl
from jax.experimental.pallas import tpu as pltpu
from jax.sharding import PartitionSpec as P

HALO = 128
COARSE = 16
LIMITS = {"far": 56, "early": 52, "pack": 52, "main": 52, "tile": 8}
LANES = 128
F32 = jnp.float32
BF16 = jnp.bfloat16


def matmul(a, b):
    return jnp.dot(a, b, preferred_element_type=F32)


def silu(v):
    return v / (1.0 + jnp.exp(-v))


def norm_rows(values, gain_row, shift_row):
    average = jnp.mean(values, axis=-1, keepdims=True)
    centered = values - average
    variance = jnp.mean(centered * centered, axis=-1, keepdims=True)
    return centered * lax.rsqrt(variance + 1e-05) * gain_row + shift_row


def column(row):
    shape = (LANES, LANES)
    same = lax.broadcasted_iota(jnp.int32, shape, 0) == lax.broadcasted_iota(jnp.int32, shape, 1)
    return jnp.sum(jnp.where(same, row.astype(F32), 0.0), axis=1, keepdims=True)


def columns(rows):
    return jnp.concatenate([column(rows[i : i + 1]) for i in range(rows.shape[0])], axis=0)


def pick(index_column, count):
    shape = (index_column.shape[0], count)
    places = lax.broadcasted_iota(jnp.int32, shape, 1).astype(F32)
    return jnp.where(places == index_column, 1.0, 0.0).astype(BF16)


def spread(index_rows, repeat):
    shape = (LANES * repeat, LANES)
    line = lax.broadcasted_iota(jnp.int32, shape, 0)
    patch = lax.broadcasted_iota(jnp.int32, shape, 1)
    here = lax.div(line, repeat) == patch
    odd = lax.rem(line, 2) == 1
    values = jnp.where(odd, index_rows[1:2].astype(F32), index_rows[0:1].astype(F32))
    return jnp.sum(jnp.where(here, values, 0.0), axis=1, keepdims=True)


def fetch(pairs, sems, first=0):
    copies = [pltpu.make_async_copy(a, b, sems.at[first + i]) for i, (a, b) in enumerate(pairs)]
    for copy in copies:
        copy.start()
    return copies


def far_kernel(nodes_hbm, rows_hbm, far_ref, inner_ref, outer_ref, nodes, index, sems):
    copies = fetch([(rows_hbm, index), (nodes_hbm, nodes)], sems)
    copies[0].wait()
    hot = pick(spread(index[...], 2), COARSE)
    copies[1].wait()
    odd = lax.rem(lax.axis_index("patch"), 2)
    span = nodes.shape[0] - HALO
    inner_ref[...] = nodes[pl.ds(pl.multiple_of((1 - odd) * span, HALO), HALO), :]
    outer_ref[...] = nodes[pl.ds(pl.multiple_of(odd * span, HALO), HALO), :]
    far_ref[...] = matmul(hot, nodes[:COARSE, :]).astype(BF16)


def early_kernel(*refs, count, vectors):
    sources, (pre_ref, send_hot, far_hot, recv_hot, recv_cold, vec_ref) = (refs[:count], refs[count : count + 6])
    places, sems = (refs[count + 6 : -1], refs[-1])
    latent = pre_ref.shape[1]
    sources = list(sources)
    sources[0] = sources[0].at[:latent]
    order = list(range(3 + 1, count)) + [0, 3, 1, 2]
    copies = {i: pltpu.make_async_copy(sources[i], places[i], sems.at[i]) for i in order}
    for i in order:
        copies[i].start()
    w_self, short, long, b_in, short_send, short_recv, long_send, long_recv = places[:8]
    for i in range(4, count):
        copies[i].wait()
    for i in range(vectors):
        vec_ref[i : i + 1, :] = places[8 + i][...]
    shorts = short.shape[0]
    quarter = recv_hot.shape[1]
    send_hot[...] = pick(columns(short_send[...]), send_hot.shape[1])
    far_hot[...] = pick(columns(long_send[...]), far_hot.shape[1])
    recv_hot[:shorts, :] = pick(columns(short_recv[...]), quarter)
    recv_hot[shorts:, :] = pick(columns(long_recv[...]), quarter)
    receivers = [short_recv[i : i + 1, :] for i in range(short_recv.shape[0])]
    receivers += [long_recv[i : i + 1, :] for i in range(long_recv.shape[0])]
    for i, receiver in enumerate(receivers):
        mine = lax.broadcasted_iota(jnp.int32, (quarter, LANES), 0) == receiver
        recv_cold[:, i * LANES : (i + 1) * LANES] = jnp.where(mine, 1.0, 0.0).astype(BF16)
    for i in range(4):
        copies[i].wait()
    pre_ref[:shorts, :] = matmul(short[...], w_self[...]) + b_in[...]
    pre_ref[shorts:, :] = matmul(long[...], w_self[...]) + b_in[...]


def pack_kernel(nodes_hbm, inner_hbm, outer_hbm, far_hbm, out_hbm, sems):
    rows = nodes_hbm.shape[0]
    ends = HALO + rows
    odd = lax.rem(lax.axis_index("patch"), 2)
    inner = pl.multiple_of((1 - odd) * ends, HALO)
    outer = pl.multiple_of(odd * ends, HALO)
    pairs = []
    for c in range(out_hbm.shape[0]):
        pairs += [
            (far_hbm, out_hbm.at[c, pl.ds(ends + HALO, far_hbm.shape[0])]),
            (nodes_hbm, out_hbm.at[c, pl.ds(HALO, rows)]),
            (inner_hbm, out_hbm.at[c, pl.ds(inner, HALO)]),
            (outer_hbm, out_hbm.at[c, pl.ds(outer, HALO)]),
        ]
    for copy in fetch(pairs, sems):
        copy.wait()


def main_kernel(*refs, count):
    sources, (short_new_hbm, long_new_hbm, own_new_ref) = (refs[:count], refs[count : count + 3])
    places, (new_edges, sems) = (refs[count + 3 : -2], refs[-2:])
    full, send_hot, w_in, recv_hot, pre, far_hot, vec, w_out, short, long, recv_cold, node_w, node_w_out = places
    chunks, quarter, width = own_new_ref.shape
    latent = chunks * width
    copies = []
    for i in range(1, count):
        source = sources[i].at[latent:] if places[i] is w_in else sources[i]
        copies.append(pltpu.make_async_copy(source, places[i], sems.at[i]))
    first = [
        pltpu.make_async_copy(sources[0].at[c], full.at[:, pl.ds(c * width, width)], sems.at[count + c])
        for c in range(chunks)
    ]
    for copy in first + copies:
        copy.start()

    def ready(*wanted):
        for i, place in enumerate(places):
            if any(place is w for w in wanted):
                copies[i - 1].wait()

    shorts, near = send_hot.shape
    for copy in first:
        copy.wait()
    start = pl.multiple_of(lax.axis_index("lat") * quarter + HALO, quarter)
    own = full[pl.ds(start, quarter), :]
    ready(send_hot, far_hot, recv_hot)
    sents = (
        matmul(send_hot[...], full[:near, :]).astype(BF16),
        matmul(far_hot[...], full[near:, :]).astype(BF16),
    )
    received = matmul(recv_hot[...], own).astype(BF16)
    ready(w_in, pre, vec, w_out, short, long)
    b_out, gain, shift, node_b, node_b_out, node_gain, node_shift = (vec[i : i + 1, :] for i in range(7))
    parts = ((0, shorts, short, short_new_hbm), (shorts, pre.shape[0], long, long_new_hbm))
    stores = []
    for i, (low, high, edges, out_hbm) in enumerate(parts):
        before = pre[low:high, :] + matmul(sents[i], w_in[:latent, :]) + matmul(received[low:high], w_in[latent:, :])
        output = matmul(silu(before).astype(BF16), w_out[...]) + b_out
        new = edges[...].astype(F32) + norm_rows(output, gain, shift)
        new_edges[low:high, :] = new.astype(BF16)
        stores.append(pltpu.make_async_copy(new_edges.at[low:high], out_hbm, sems.at[count + chunks + i]))
        stores[-1].start()
    ready(recv_cold, node_w, node_w_out)
    aggregate = matmul(recv_cold[...], new_edges[...]).astype(BF16)
    node_pre = matmul(own, node_w[:latent, :]) + matmul(aggregate, node_w[latent:, :]) + node_b
    node_out = matmul(silu(node_pre).astype(BF16), node_w_out[...]) + node_b_out
    new = own.astype(F32) + norm_rows(node_out, node_gain, node_shift)
    new = new.astype(BF16)
    for c in range(chunks):
        own_new_ref[c] = new[:, c * width : (c + 1) * width]
    for copy in stores:
        copy.wait()


def tile_kernel(rows_ref, index_ref, out_ref):
    hot = pick(spread(index_ref[...], 2), rows_ref.shape[0])
    out_ref[...] = matmul(hot, rows_ref[...]).astype(BF16)


VMEM = pl.BlockSpec(memory_space=pltpu.VMEM)
ANY = pl.BlockSpec(memory_space=pl.ANY)
DMA = pltpu.SemaphoreType.DMA


def call(kernel, operands, outs, limit, flops, scratch=(), ins=ANY, out_specs=None):
    return pl.pallas_call(
        kernel,
        out_shape=tuple(outs),
        in_specs=[ins] * len(operands),
        out_specs=tuple(out_specs or [VMEM] * len(outs)),
        scratch_shapes=list(scratch),
        compiler_params=pltpu.CompilerParams(vmem_limit_bytes=limit * 1024 * 1024),
        cost_estimate=pl.CostEstimate(flops=flops, bytes_accessed=0, transcendentals=0),
    )(*operands)


def shape(dims, dtype=BF16):
    return jax.ShapeDtypeStruct(dims, dtype)


def like(arrays):
    return [pltpu.VMEM(x.shape, x.dtype) for x in arrays]


def body(
    nodes,
    short_edges,
    long_edges,
    short_send,
    short_recv,
    long_send,
    long_recv,
    send_rows,
    tile_rows,
    edge_w_in,
    edge_b_in,
    edge_w_out,
    edge_b_out,
    edge_gain,
    edge_shift,
    node_w_in,
    node_b_in,
    node_w_out,
    node_b_out,
    node_gain,
    node_shift,
):
    latent = edge_w_out.shape[0]
    rows, width = nodes.shape
    patches, lats = lax.axis_size("patch"), lax.axis_size("lat")
    slots = send_rows.shape[2]
    quarter = rows // lats
    shorts, longs = short_edges.shape[0], long_edges.shape[0]
    edges = shorts + longs
    near, far = rows + 2 * HALO, patches * slots

    outgoing, inner, outer = call(
        far_kernel,
        [nodes, send_rows[0].T],
        [shape((far, width)), shape((HALO, width)), shape((HALO, width))],
        LIMITS["far"],
        2 * far * COARSE * width,
        [pltpu.VMEM((rows, width), BF16), pltpu.VMEM((slots, patches), jnp.int32), DMA((2,))],
    )
    arrived = lax.all_to_all(
        outgoing.reshape(patches, slots, width), "patch", split_axis=0, concat_axis=0, tiled=True
    ).reshape(far, width)
    inner = lax.ppermute(inner, "patch", [(i, i ^ 1) for i in range(patches)])
    outer = lax.ppermute(outer, "patch", [(i, ((i + 1) ^ 1) - 1) for i in range(1, patches - 1)] + [(0, patches - 1), (patches - 1, 0)])
    (packed,) = call(
        pack_kernel,
        [nodes, inner, outer, arrived],
        [shape((lats, near + far, width))],
        LIMITS["pack"],
        0,
        [DMA((4 * lats,))],
        out_specs=[ANY],
    )
    full = lax.all_to_all(packed, "lat", split_axis=0, concat_axis=0, tiled=True)

    vectors = [v.reshape(1, latent) for v in (edge_b_out, edge_gain, edge_shift, node_b_in, node_b_out, node_gain, node_shift)]
    ints = [v.reshape(-1, LANES) for v in (short_send, short_recv, long_send, long_recv)]
    sources = [edge_w_in, short_edges, long_edges, edge_b_in.reshape(1, latent), *ints, *vectors]
    pre, send_hot, far_hot, recv_hot, recv_cold, vec = call(
        functools.partial(early_kernel, count=len(sources), vectors=len(vectors)),
        sources,
        [
            shape((edges, latent), F32),
            shape((shorts, near)),
            shape((longs, far)),
            shape((edges, quarter)),
            shape((quarter, edges)),
            shape((8, latent), F32),
        ],
        LIMITS["early"],
        2 * edges * latent * latent,
        [pltpu.VMEM((latent, latent), BF16)] + like(sources[1:]) + [DMA((len(sources),))],
    )
    sources = [full, send_hot, edge_w_in, recv_hot, pre, far_hot, vec, edge_w_out, short_edges, long_edges, recv_cold]
    sources += [node_w_in, node_w_out]
    places = [pltpu.VMEM((near + far, latent), BF16)] + like(sources[1:])
    places[2] = pltpu.VMEM((2 * latent, latent), BF16)
    short_new, long_new, own_new = call(
        functools.partial(main_kernel, count=len(sources)),
        sources,
        [shape((shorts, latent)), shape((longs, latent)), shape((lats, quarter, width))],
        LIMITS["main"],
        2 * edges * latent * latent * 5,
        places + [pltpu.VMEM((edges, latent), BF16), DMA((len(sources) + lats + 2,))],
        out_specs=[ANY, ANY, VMEM],
    )
    node_rows = lax.all_to_all(own_new, "lat", split_axis=0, concat_axis=0, tiled=True).reshape(rows, width)
    (tile_send,) = call(
        tile_kernel,
        [node_rows, tile_rows[0].T],
        [shape((far, width))],
        LIMITS["tile"],
        2 * far * rows * width,
        ins=VMEM,
    )
    tiles = lax.all_to_all(
        tile_send.reshape(patches, slots, width), "patch", split_axis=0, concat_axis=0, tiled=True
    ).reshape(far, width)

    return (short_new, long_new, node_rows, tiles)


def solution(mesh):
    placed = (
        P("patch", "lat"),
        P(("patch", "lat"), None),
        P(("patch", "lat"), None),
        P(("patch", "lat")),
        P(("patch", "lat")),
        P(("patch", "lat")),
        P(("patch", "lat")),
        P("patch", None, None),
        P("patch", None, None),
    ) + (P(),) * 12
    return jax.shard_map(
        body,
        mesh=mesh,
        in_specs=placed,
        out_specs=(
            P(("patch", "lat"), None),
            P(("patch", "lat"), None),
            P("patch", "lat"),
            P("patch", "lat"),
        ),
        check_vma=False,
    )
```

time: 97 us -> 87.7 us (0.904)
  blocking collectives: 10.6 us -> 30.7 us
  starting transfers between devices: 39.3 us -> 28.2 us
  Pallas kernels: 0 us -> 8.74 us
  matrix products: 8.07 us -> 0 us
  local copies, waits for them, and re-layouts: 11.7 us -> 4 us
  waiting for transfers between devices: 21.3 us -> 14.7 us
  other arithmetic: 4.32 us -> 0 us
    all_to_all x0 -> x2, blocking collectives: none -> 30.7 us  [the longest x1 23.8 us: body(): lax.all_to_all(tile_send.reshape(patches, slots, width), 'patch', split_a...]
    all_gather x1 -> x0, blocking collectives: 10.6 us -> none  [body(): full_rows = lax.all_gather(nodes, 'lat', axis=1, tiled=True)]
    all_to_all x3 -> x2, waiting for transfers between devices: 21.3 us -> 11.7 us  [the longest x1 8.91 us: body(): lax.all_to_all(packed, 'lat', split_axis=0, concat_axis=0, tiled=True)]
    pallas_call x0 -> x5, Pallas kernels: none -> 8.74 us  [call(): pl.pallas_call(kernel, out_shape=tuple(outs), in_specs=[ins] * len(operan...]
    dot_general x7 -> x0, matrix products: 8.07 us -> none  [the longest x1 1.87 us: body(): jnp.dot(hidden, edge_w_out, preferred_element_type=jnp.float32) + edge_b_out]
    gather x7 -> x0, local copies, waits for them, and re-layouts: 6.26 us -> none  [the longest x1 1.45 us: body(): jnp.take(recv_proj, long_recv, axis=0)]
    ppermute x2, starting transfers between devices: 11.5 us -> 5.6 us  [the longest x1 2.8 us: body(): inner = lax.ppermute(inner, 'patch', [(i, i ^ 1) for i in range(patches)])]
    all_to_all x3 -> x2, starting transfers between devices: 27.7 us -> 22.6 us  [the longest x1 18.4 us: body(): lax.all_to_all(outgoing.reshape(patches, slots, width), 'patch', split_ax...]
  transfers between devices with their start and end apart: 5 -> 4, of which waited for: 3 -> 3; matrix products, arithmetic and copies ran while one was open for 13% -> 0% of each run, Pallas kernels for 0% -> 2%
where the time goes in v2:
time: 87.7 us; the launch traced here: 87.3 us
  blocking collectives  30.7 us (35%)
  starting transfers between devices  28.2 us (32%)
  waiting for transfers between devices  14.7 us (17%)
  Pallas kernels  8.74 us (10%)
  local copies, waits for them, and re-layouts  4 us (5%)
  between operations  0.91 us (1%)
    all_to_all x1, blocking collectives, body(): lax.all_to_all(tile_send.reshape(patches, slots, width), 'patch', split_a...  23.8 us
    all_to_all x1, starting transfers between devices, body(): lax.all_to_all(outgoing.reshape(patches, slots, width), 'patch', split_ax...  18.4 us
    all_to_all x1, waiting for transfers between devices, body(): lax.all_to_all(packed, 'lat', split_axis=0, concat_axis=0, tiled=True)  8.91 us
    pallas_call x5, Pallas kernels, call(): pl.pallas_call(kernel, out_shape=tuple(outs), in_specs=[ins] * len(operan...  8.74 us
    all_to_all x1, blocking collectives, body(): lax.all_to_all(own_new, 'lat', split_axis=0, concat_axis=0, tiled=True)  6.84 us
    all_to_all x1, starting transfers between devices, body(): lax.all_to_all(packed, 'lat', split_axis=0, concat_axis=0, tiled=True)  4.15 us
    unnamed x42, local copies, waits for them, and re-layouts  4 us
    ppermute x1, waiting for transfers between devices, body(): lax.ppermute(outer, 'patch', [(i, (i + 1 ^ 1) - 1) for i in range(1, patc...  3 us
  transfers between devices with their start and end apart: 4, of which 3 were waited for; matrix products, arithmetic and copies ran while one was open for 0% of the time, Pallas kernels for 2%

profile of v2, /device:TPU:1, one launch (start us, length us, event | category | flops | bytes accessed | tf_op | source)
XLA Modules:
  0.0 87.3 jit_solution(16838413028631353776)
XLA Ops:
  0.6 0.0 copy-start.4
  0.6 0.0 copy-start
  0.7 1.7 %shard_map.228 = (bf16[256,128]{1,0:T(8,128)(2,1)}, bf16[128,128]{1,0:T(8,128)(2,1)}, bf16[128,128]{1,0:T(8,128)(2,1)}) custom-call(bf16[256,128]{1,0:T(8,128)(2,1)} %nodes_hbm.3, s32[2,128]{1,0:T(2,128)} %bitcast.42), custom_call_target="tpu_custom_call" | custom-call | flops 1048576 | tf_op jit(solution)/shard_map/pallas_call | solution.py:195
  2.4 18.4 %all-to-all-start = ((bf16[128,2,128]{2,1,0:T(2,128)(2,1)}), bf16[128,2,128]{2,1,0:T(2,128)(2,1)S(1)}, u32[]{:S(2)}, u32[]{:S(2)}) async-start(bf16[128,2,128]{2,1,0:T(2,128)(2,1)} %bitcast.41), calls=%async_computation | async-start | bytes 131072 | tf_op jit(solution)/shard_map/all_to_all | solution.py:254
  20.8 2.8 %collective-permute-start = (bf16[128,128]{1,0:T(8,128)(2,1)}, bf16[128,128]{1,0:T(8,128)(2,1)S(1)}, u32[]{:S(2)}, u32[]{:S(2)}) collective-permute-start(bf16[128,128]{1,0:T(8,128)(2,1)} %get-tuple-element.16), channel_id=1, source_target_pairs={{0,4},{4,0},{8,12},{12,8},{16,20},{20,16},{24,28},{28,24},{32,36},... | collective-permute-start | bytes 98312 | tf_op jit(solution)/shard_map/ppermute | solution.py:257
  23.6 2.8 %collective-permute-start.1 = (bf16[128,128]{1,0:T(8,128)(2,1)}, bf16[128,128]{1,0:T(8,128)(2,1)S(1)}, u32[]{:S(2)}, u32[]{:S(2)}) collective-permute-start(bf16[128,128]{1,0:T(8,128)(2,1)} %get-tuple-element.17), channel_id=1, source_target_pairs={{4,8},{8,4},{12,16},{16,12},{20,24},{24,20},{28,32},{32,28},{36,40... | collective-permute-start | bytes 98312 | tf_op jit(solution)/shard_map/ppermute | solution.py:258
  26.4 0.0 collective-permute-done.inner_hbm
  26.4 3.0 %collective-permute-done.1.outer_hbm = bf16[128,128]{1,0:T(8,128)(2,1)S(1)} collective-permute-done((bf16[128,128]{1,0:T(8,128)(2,1)}, bf16[128,128]{1,0:T(8,128)(2,1)S(1)}, u32[]{:S(2)}, u32[]{:S(2)}) %collective-permute-start.1) | collective-permute-done | bytes 32800 | tf_op jit(solution)/shard_map/ppermute | solution.py:258
  29.4 2.8 %all-to-all-done = bf16[128,2,128]{2,1,0:T(2,128)(2,1)S(1)} async-done(((bf16[128,2,128]{2,1,0:T(2,128)(2,1)}), bf16[128,2,128]{2,1,0:T(2,128)(2,1)S(1)}, u32[]{:S(2)}, u32[]{:S(2)}) %all-to-all-start) | async-done | bytes 65568 | tf_op jit(solution)/shard_map/all_to_all | solution.py:254
  32.2 0.8 copy-done.5
  33.1 0.0 copy-start.10
  33.1 0.0 copy-start.11
  33.1 0.0 copy-start.12
  33.1 0.0 copy-start.13
  33.1 0.0 copy-start.14
  33.2 0.0 copy-start.15
  33.2 0.0 copy-start.17
  33.2 0.0 copy-start.18
  33.2 1.1 %shard_map.229 = bf16[4,768,128]{2,1,0:T(8,128)(2,1)} custom-call(bf16[256,128]{1,0:T(8,128)(2,1)S(1)} %copy-done.5, bf16[128,128]{1,0:T(8,128)(2,1)S(1)} %collective-permute-done.inner_hbm, bf16[128,128]{1,0:T(8,128)(2,1)S(1)} %collective-permute-done.1.outer_hbm, bf16[256,128]{1,0:T(8,128)(2,1)S(1)} %bitcast.26), custom_call_target="tpu_custom_call" | custom-call | tf_op jit(solution)/shard_map/pallas_call | solution.py:195
  34.3 0.0 copy-start.2
  34.3 0.0 copy-start.3
  34.3 4.2 %all-to-all-start.1 = ((bf16[4,768,128]{2,1,0:T(8,128)(2,1)}), bf16[4,768,128]{2,1,0:T(8,128)(2,1)S(1)}, u32[]{:S(2)}, u32[]{:S(2)}) async-start(bf16[4,768,128]{2,1,0:T(8,128)(2,1)} %shard_map.229), calls=%async_computation.1 | async-start | bytes 1572864 | tf_op jit(solution)/shard_map/all_to_all | solution.py:268
  38.4 0.0 copy-done.4
  38.4 0.0 copy-done
  38.4 0.0 copy-done.6
  38.4 0.0 copy-done.7
  38.5 0.0 copy-done.8
  38.5 0.0 copy-done.9
  38.5 0.0 copy-done.10
  38.5 0.0 copy-done.11
  38.5 0.0 copy-done.12
  38.5 0.0 copy-done.13
  38.5 0.0 copy-done.14
  38.5 0.0 copy-done.15
  38.5 0.0 copy-done.17
  38.5 0.0 copy-done.18
  38.6 1.6 %shard_map.230 = (f32[384,512]{1,0:T(8,128)S(1)}, bf16[256,512]{1,0:T(8,128)(2,1)S(1)}, bf16[128,256]{1,0:T(8,128)(2,1)S(1)}, bf16[384,64]{1,0:T(8,128)(2,1)S(1)...) custom-call(bf16[1536,512]{1,0:T(8,128)(2,1)} %refs_2_.3, bf16[256,512]{1,0:T(8,128)(2,1)S(1)} %copy-done, ...), custom_call_target="tpu_custom_call" | custom-call | flops 201326592 | tf_op jit(solution)/shard_map/pallas_call | solution.py:195
  40.1 0.0 copy-start.1
  40.2 0.9 %copy-done.1 = f32[384,512]{1,0:T(8,128)} copy-done((f32[384,512]{1,0:T(8,128)}, f32[384,512]{1,0:T(8,128)S(1)}, u32[]{:S(2)}) %copy-start.1) | copy-done | bytes 786456
  41.0 8.9 %all-to-all-done.1.refs_0_ = bf16[4,768,128]{2,1,0:T(8,128)(2,1)S(1)} async-done(((bf16[4,768,128]{2,1,0:T(8,128)(2,1)}), bf16[4,768,128]{2,1,0:T(8,128)(2,1)S(1)}, u32[]{:S(2)}, u32[]{:S(2)}) %all-to-all-start.1) | async-done | bytes 786464 | tf_op jit(solution)/shard_map/all_to_all | solution.py:268
  50.0 0.9 %copy-done.19 = bf16[4,768,128]{2,1,0:T(8,128)(2,1)} copy-done((bf16[4,768,128]{2,1,0:T(8,128)(2,1)}, bf16[4,768,128]{2,1,0:T(8,128)(2,1)S(1)}, u32[]{:S(2)}) %copy-start.19) | copy-done | bytes 786456
  50.9 4.2 %shard_map.231 = (bf16[256,512]{1,0:T(8,128)(2,1)}, bf16[128,512]{1,0:T(8,128)(2,1)}, bf16[4,64,128]{2,1,0:T(8,128)(2,1)S(1)}) custom-call(bf16[4,768,128]{2,1,0:T(8,128)(2,1)} %copy-done.19, bf16[256,512]{1,0:T(8,128)(2,1)S(1)} %get-tuple-element.19.refs_1_, bf16[1536,512]{1,0:T(8,128)(2,1)} %refs_2_.3, bf16[384,64]{1,0:T(8,128)(2,1)S(1)} %get-tuple-element.20.refs_3_, ...), custom_call_target="tpu_custom_call" | custom-call | flops 1006632960 | tf_op jit(solution)/shard_map/pallas_call | solution.py:195
  55.1 6.8 %all_to_all.20 = bf16[4,64,128]{2,1,0:T(8,128)(2,1)S(1)} all-to-all(bf16[4,64,128]{2,1,0:T(8,128)(2,1)S(1)} %get-tuple-element.27), channel_id=1, replica_groups=mesh['patch'=128,'lat'=4] {'lat'}, dimensions={0} | all-to-all | bytes 131072 | tf_op jit(solution)/shard_map/all_to_all | solution.py:301
  61.9 0.0 copy-done.16
  61.9 0.2 shard_map.232
  62.1 23.8 %all_to_all.21 = bf16[128,2,128]{2,1,0:T(2,128)(2,1)S(1)} all-to-all(bf16[128,2,128]{2,1,0:T(2,128)(2,1)S(1)} %bitcast.25), channel_id=1, replica_groups=mesh['patch'=128,'lat'=4] {'patch'}, dimensions={0} | all-to-all | bytes 131072 | tf_op jit(solution)/shard_map/all_to_all | solution.py:310
  86.0 0.6 copy.27
  86.6 0.6 copy.28
  (9 shorter events, 0.0 us)
Async XLA Ops:
  0.6 37.8 %copy-start.4 = (bf16[128,512]{1,0:T(8,128)(2,1)S(1)}, bf16[128,512]{1,0:T(8,128)(2,1)}, u32[]{:S(2)}) copy-start(bf16[128,512]{1,0:T(8,128)(2,1)} %refs_9_.1) | copy-start | bytes 393220
  0.6 37.8 %copy-start = (bf16[256,512]{1,0:T(8,128)(2,1)S(1)}, bf16[256,512]{1,0:T(8,128)(2,1)}, u32[]{:S(2)}) copy-start(bf16[256,512]{1,0:T(8,128)(2,1)} %refs_8_.1) | copy-start | bytes 786436
  2.4 29.9 %all-to-all-start = ((bf16[128,2,128]{2,1,0:T(2,128)(2,1)}), bf16[128,2,128]{2,1,0:T(2,128)(2,1)S(1)}, u32[]{:S(2)}, u32[]{:S(2)}) async-start(bf16[128,2,128]{2,1,0:T(2,128)(2,1)} %bitcast.41), calls=%async_computation | async-start | bytes 131072 | tf_op jit(solution)/shard_map/all_to_all | solution.py:254
  20.8 5.6 %collective-permute-start = (bf16[128,128]{1,0:T(8,128)(2,1)}, bf16[128,128]{1,0:T(8,128)(2,1)S(1)}, u32[]{:S(2)}, u32[]{:S(2)}) collective-permute-start(bf16[128,128]{1,0:T(8,128)(2,1)} %get-tuple-element.16), channel_id=1, source_target_pairs={{0,4},{4,0},{8,12},{12,8},{16,20},{20,16},{24,28},{28,24},{32,36},... | collective-permute-start | bytes 98312 | tf_op jit(solution)/shard_map/ppermute | solution.py:257
  23.6 5.8 %collective-permute-start.1 = (bf16[128,128]{1,0:T(8,128)(2,1)}, bf16[128,128]{1,0:T(8,128)(2,1)S(1)}, u32[]{:S(2)}, u32[]{:S(2)}) collective-permute-start(bf16[128,128]{1,0:T(8,128)(2,1)} %get-tuple-element.17), channel_id=1, source_target_pairs={{4,8},{8,4},{12,16},{16,12},{20,24},{24,20},{28,32},{32,28},{36,40... | collective-permute-start | bytes 98312 | tf_op jit(solution)/shard_map/ppermute | solution.py:258
  32.2 0.8 copy-start.5
  33.1 5.4 %copy-start.6 = (f32[512]{0:T(512)S(1)}, f32[512]{0:T(512)}, u32[]{:S(2)}) copy-start(f32[512]{0:T(512)} %param.31) | copy-start | bytes 6148
  33.1 5.4 %copy-start.7 = (f32[512]{0:T(512)S(1)}, f32[512]{0:T(512)}, u32[]{:S(2)}) copy-start(f32[512]{0:T(512)} %param.33) | copy-start | bytes 6148
  33.1 5.4 %copy-start.8 = (f32[512]{0:T(512)S(1)}, f32[512]{0:T(512)}, u32[]{:S(2)}) copy-start(f32[512]{0:T(512)} %param.34) | copy-start | bytes 6148
  33.1 5.4 %copy-start.9 = (f32[512]{0:T(512)S(1)}, f32[512]{0:T(512)}, u32[]{:S(2)}) copy-start(f32[512]{0:T(512)} %param.35) | copy-start | bytes 6148
  33.1 5.4 %copy-start.10 = (f32[512]{0:T(512)S(1)}, f32[512]{0:T(512)}, u32[]{:S(2)}) copy-start(f32[512]{0:T(512)} %param.37) | copy-start | bytes 6148
  33.1 5.4 %copy-start.11 = (f32[512]{0:T(512)S(1)}, f32[512]{0:T(512)}, u32[]{:S(2)}) copy-start(f32[512]{0:T(512)} %param.39) | copy-start | bytes 6148
  33.1 5.4 %copy-start.12 = (f32[512]{0:T(512)S(1)}, f32[512]{0:T(512)}, u32[]{:S(2)}) copy-start(f32[512]{0:T(512)} %param.40) | copy-start | bytes 6148
  33.1 5.4 %copy-start.13 = (f32[512]{0:T(512)S(1)}, f32[512]{0:T(512)}, u32[]{:S(2)}) copy-start(f32[512]{0:T(512)} %param.41) | copy-start | bytes 6148
  33.1 5.4 %copy-start.14 = (s32[256]{0:T(256)S(1)}, s32[256]{0:T(256)}, u32[]{:S(2)}) copy-start(s32[256]{0:T(256)} %param.24) | copy-start | bytes 3076
  33.2 5.4 %copy-start.15 = (s32[256]{0:T(256)S(1)}, s32[256]{0:T(256)}, u32[]{:S(2)}) copy-start(s32[256]{0:T(256)} %param.25) | copy-start | bytes 3076
  33.2 5.4 %copy-start.17 = (s32[128]{0:T(128)S(1)}, s32[128]{0:T(128)}, u32[]{:S(2)}) copy-start(s32[128]{0:T(128)} %param.26) | copy-start | bytes 1540
  33.2 5.4 %copy-start.18 = (s32[128]{0:T(128)S(1)}, s32[128]{0:T(128)}, u32[]{:S(2)}) copy-start(s32[128]{0:T(128)} %param.27) | copy-start | bytes 1540
  34.3 16.6 %copy-start.2 = (bf16[512,512]{1,0:T(8,128)(2,1)S(1)}, bf16[512,512]{1,0:T(8,128)(2,1)}, u32[]{:S(2)}) copy-start(bf16[512,512]{1,0:T(8,128)(2,1)} %refs_7_.1) | copy-start | bytes 1572868
  34.3 16.6 %copy-start.3 = (bf16[512,512]{1,0:T(8,128)(2,1)S(1)}, bf16[512,512]{1,0:T(8,128)(2,1)}, u32[]{:S(2)}) copy-start(bf16[512,512]{1,0:T(8,128)(2,1)} %refs_12_.1) | copy-start | bytes 1572868
  34.3 15.7 %all-to-all-start.1 = ((bf16[4,768,128]{2,1,0:T(8,128)(2,1)}), bf16[4,768,128]{2,1,0:T(8,128)(2,1)S(1)}, u32[]{:S(2)}, u32[]{:S(2)}) async-start(bf16[4,768,128]{2,1,0:T(8,128)(2,1)} %shard_map.229), calls=%async_computation.1 | async-start | bytes 1572864 | tf_op jit(solution)/shard_map/all_to_all | solution.py:268
  40.1 0.9 %copy-start.1 = (f32[384,512]{1,0:T(8,128)}, f32[384,512]{1,0:T(8,128)S(1)}, u32[]{:S(2)}) copy-start(f32[384,512]{1,0:T(8,128)S(1)} %get-tuple-element.21.refs_4_) | copy-start | bytes 2359300
  49.9 0.9 %copy-start.19 = (bf16[4,768,128]{2,1,0:T(8,128)(2,1)}, bf16[4,768,128]{2,1,0:T(8,128)(2,1)S(1)}, u32[]{:S(2)}) copy-start(bf16[4,768,128]{2,1,0:T(8,128)(2,1)S(1)} %all-to-all-done.1.refs_0_) | copy-start | bytes 2359300
  50.9 11.0 %copy-start.16 = (s32[1,128,2]{1,2,0:T(2,128)S(1)}, s32[1,128,2]{1,2,0:T(2,128)}, u32[]{:S(2)}) copy-start(s32[1,128,2]{1,2,0:T(2,128)} %param.29) | copy-start | bytes 3076

commit v3 on v2

--- a/solution.py
+++ b/solution.py
@@ -9,7 +9,7 @@
 
 HALO = 128
 COARSE = 16
-LIMITS = {"far": 56, "early": 52, "pack": 52, "main": 52, "tile": 8}
+LIMITS = {"far": 56, "early": 56, "pack": 52, "main": 52, "tile": 8}
 LANES = 128
 F32 = jnp.float32
 BF16 = jnp.bfloat16
@@ -46,12 +46,16 @@
     return jnp.where(places == index_column, 1.0, 0.0).astype(BF16)
 
 
+def shift(power):
+    return power.bit_length() - 1
+
+
 def spread(index_rows, repeat):
     shape = (LANES * repeat, LANES)
     line = lax.broadcasted_iota(jnp.int32, shape, 0)
     patch = lax.broadcasted_iota(jnp.int32, shape, 1)
-    here = lax.div(line, repeat) == patch
-    odd = lax.rem(line, 2) == 1
+    here = (line >> shift(repeat)) == patch
+    odd = (line & 1) == 1
     values = jnp.where(odd, index_rows[1:2].astype(F32), index_rows[0:1].astype(F32))
     return jnp.sum(jnp.where(here, values, 0.0), axis=1, keepdims=True)
 
@@ -126,10 +130,10 @@
 
 
 def main_kernel(*refs, count):
-    sources, (short_new_hbm, long_new_hbm, own_new_ref) = (refs[:count], refs[count : count + 3])
-    places, (new_edges, sems) = (refs[count + 3 : -2], refs[-2:])
-    full, send_hot, w_in, recv_hot, pre, far_hot, vec, w_out, short, long, recv_cold, node_w, node_w_out = places
-    chunks, quarter, width = own_new_ref.shape
+    sources, (short_new_hbm, long_new_hbm, tile_ref, *own_news) = (refs[:count], refs[count : count + 7])
+    places, (new_edges, tile_hot, own_new, sems) = (refs[count + 7 : -4], refs[-4:])
+    full, send_hot, w_in, recv_hot, pre, far_hot, vec, w_out, short, long, recv_cold, node_w, node_w_out, index = places
+    chunks, quarter, width = own_new.shape
     latent = chunks * width
     copies = []
     for i in range(1, count):
@@ -148,6 +152,9 @@
                 copies[i - 1].wait()
 
     shorts, near = send_hot.shape
+    lat = lax.axis_index("lat")
+    ready(index)
+    tile_hot[...] = pick(spread(index[...], 2) - (lat * quarter).astype(F32), quarter)
     for copy in first:
         copy.wait()
     start = pl.multiple_of(lax.axis_index("lat") * quarter + HALO, quarter)
@@ -176,14 +183,29 @@
     new = own.astype(F32) + norm_rows(node_out, node_gain, node_shift)
     new = new.astype(BF16)
     for c in range(chunks):
-        own_new_ref[c] = new[:, c * width : (c + 1) * width]
+        own_new[c] = new[:, c * width : (c + 1) * width]
+    for d in range(chunks):
+        own_news[d][...] = own_new[lat ^ d]
+    tile = matmul(tile_hot[...], new).astype(BF16)
+    for c in range(chunks):
+        tile_ref[c] = tile[:, c * width : (c + 1) * width]
     for copy in stores:
         copy.wait()
 
 
-def tile_kernel(rows_ref, index_ref, out_ref):
-    hot = pick(spread(index_ref[...], 2), rows_ref.shape[0])
-    out_ref[...] = matmul(hot, rows_ref[...]).astype(BF16)
+def tile_kernel(arrived_ref, out_ref):
+    total = arrived_ref[0].astype(F32)
+    for c in range(1, arrived_ref.shape[0]):
+        total = total + arrived_ref[c].astype(F32)
+    out_ref[...] = total.astype(BF16)
+
+
+def rows_kernel(*refs):
+    pieces, out_ref = (refs[:-1], refs[-1])
+    count = len(pieces)
+    lat = lax.axis_index("lat")
+    for d in range(count):
+        out_ref[lat ^ d] = pieces[d][...]
 
 
 VMEM = pl.BlockSpec(memory_space=pltpu.VMEM)
@@ -256,17 +278,6 @@
     ).reshape(far, width)
     inner = lax.ppermute(inner, "patch", [(i, i ^ 1) for i in range(patches)])
     outer = lax.ppermute(outer, "patch", [(i, ((i + 1) ^ 1) - 1) for i in range(1, patches - 1)] + [(0, patches - 1), (patches - 1, 0)])
-    (packed,) = call(
-        pack_kernel,
-        [nodes, inner, outer, arrived],
-        [shape((lats, near + far, width))],
-        LIMITS["pack"],
-        0,
-        [DMA((4 * lats,))],
-        out_specs=[ANY],
-    )
-    full = lax.all_to_all(packed, "lat", split_axis=0, concat_axis=0, tiled=True)
-
     vectors = [v.reshape(1, latent) for v in (edge_b_out, edge_gain, edge_shift, node_b_in, node_b_out, node_gain, node_shift)]
     ints = [v.reshape(-1, LANES) for v in (short_send, short_recv, long_send, long_recv)]
     sources = [edge_w_in, short_edges, long_edges, edge_b_in.reshape(1, latent), *ints, *vectors]
@@ -285,32 +296,47 @@
         2 * edges * latent * latent,
         [pltpu.VMEM((latent, latent), BF16)] + like(sources[1:]) + [DMA((len(sources),))],
     )
+    arrived, pre, send_hot, far_hot, recv_hot, recv_cold, vec = lax.optimization_barrier(
+        (arrived, pre, send_hot, far_hot, recv_hot, recv_cold, vec)
+    )
+    (packed,) = call(
+        pack_kernel,
+        [nodes, inner, outer, arrived],
+        [shape((lats, near + far, width))],
+        LIMITS["pack"],
+        0,
+        [DMA((4 * lats,))],
+        out_specs=[ANY],
+    )
+    full = lax.all_to_all(packed, "lat", split_axis=0, concat_axis=0, tiled=True)
+
     sources = [full, send_hot, edge_w_in, recv_hot, pre, far_hot, vec, edge_w_out, short_edges, long_edges, recv_cold]
-    sources += [node_w_in, node_w_out]
+    sources += [node_w_in, node_w_out, tile_rows[0].T]
     places = [pltpu.VMEM((near + far, latent), BF16)] + like(sources[1:])
     places[2] = pltpu.VMEM((2 * latent, latent), BF16)
-    short_new, long_new, own_new = call(
+    short_new, long_new, tile_send, *pieces = call(
         functools.partial(main_kernel, count=len(sources)),
         sources,
-        [shape((shorts, latent)), shape((longs, latent)), shape((lats, quarter, width))],
+        [shape((shorts, latent)), shape((longs, latent)), shape((lats, far, width))] + [shape((quarter, width))] * lats,
         LIMITS["main"],
         2 * edges * latent * latent * 5,
-        places + [pltpu.VMEM((edges, latent), BF16), DMA((len(sources) + lats + 2,))],
-        out_specs=[ANY, ANY, VMEM],
-    )
-    node_rows = lax.all_to_all(own_new, "lat", split_axis=0, concat_axis=0, tiled=True).reshape(rows, width)
-    (tile_send,) = call(
-        tile_kernel,
-        [node_rows, tile_rows[0].T],
-        [shape((far, width))],
-        LIMITS["tile"],
-        2 * far * rows * width,
-        ins=VMEM,
-    )
-    tiles = lax.all_to_all(
-        tile_send.reshape(patches, slots, width), "patch", split_axis=0, concat_axis=0, tiled=True
-    ).reshape(far, width)
-
+        places
+        + [
+            pltpu.VMEM((edges, latent), BF16),
+            pltpu.VMEM((far, quarter), BF16),
+            pltpu.VMEM((lats, quarter, width), BF16),
+            DMA((len(sources) + lats + 2,)),
+        ],
+        out_specs=[ANY, ANY] + [VMEM] * (1 + lats),
+    )
+    arrived = lax.all_to_all(
+        tile_send.reshape(lats * patches, slots, width), ("lat", "patch"), split_axis=0, concat_axis=0, tiled=True
+    ).reshape(lats, far, width)
+    for d in range(1, lats):
+        pieces[d] = lax.ppermute(pieces[d], "lat", [(i, i ^ d) for i in range(lats)])
+    (node_rows,) = call(rows_kernel, pieces, [shape((lats, quarter, width))], 8, 10**9, ins=VMEM)
+    node_rows = node_rows.reshape(rows, width)
+    (tiles,) = call(tile_kernel, [arrived], [shape((far, width))], 8, 10**8, ins=VMEM)
     return (short_new, long_new, node_rows, tiles)
 
 

time: 87.7 us -> 85.1 us (0.970)
  starting transfers between devices: 28.2 us -> 47.7 us
  blocking collectives: 30.7 us -> 14.5 us
  waiting for transfers between devices: 14.7 us -> 9.57 us
  local copies, waits for them, and re-layouts: 4 us -> 0.06 us
  Pallas kernels: 8.74 us -> 12 us
    all_to_all x2 -> x1, blocking collectives: 30.7 us -> 14.5 us  [body(): lax.all_to_all(packed, 'lat', split_axis=0, concat_axis=0, tiled=True)]
    all_to_all x1, starting transfers between devices: 4.15 us -> 14.1 us  [body(): lax.all_to_all(tile_send.reshape(lats * patches, slots, width), ('lat', '...]
    ppermute x0 -> x3, starting transfers between devices: none -> 9.58 us  [body(): lax.ppermute(pieces[d], 'lat', [(i, i ^ d) for i in range(lats)])]
    all_to_all x1, waiting for transfers between devices: 8.91 us -> 2.51 us  [body(): lax.all_to_all(tile_send.reshape(lats * patches, slots, width), ('lat', '...]
    ppermute x0 -> x3, waiting for transfers between devices: none -> 4.01 us  [body(): lax.ppermute(pieces[d], 'lat', [(i, i ^ d) for i in range(lats)])]
    unnamed x42 -> x20, local copies, waits for them, and re-layouts: 4 us -> 0.06 us
    pallas_call x5 -> x6, Pallas kernels: 8.74 us -> 12 us  [call(): pl.pallas_call(kernel, out_shape=tuple(outs), in_specs=[ins] * len(operan...]
    ppermute x1, waiting for transfers between devices: 3 us -> 0.01 us  [body(): lax.ppermute(outer, 'patch', [(i, (i + 1 ^ 1) - 1) for i in range(1, patc...]
  transfers between devices with their start and end apart: 4 -> 7, of which waited for: 3 -> 3; matrix products, arithmetic and copies ran while one was open for 0% -> 0% of each run, Pallas kernels for 2% -> 4%
where the time goes in v3:
time: 85.1 us; the launch traced here: 84.7 us
  starting transfers between devices  47.7 us (56%)
  blocking collectives  14.5 us (17%)
  Pallas kernels  12 us (14%)
  waiting for transfers between devices  9.57 us (11%)
  between operations  0.86 us (1%)
    all_to_all x1, starting transfers between devices, body(): lax.all_to_all(outgoing.reshape(patches, slots, width), 'patch', split_ax...  18.4 us
    all_to_all x1, blocking collectives, body(): lax.all_to_all(packed, 'lat', split_axis=0, concat_axis=0, tiled=True)  14.5 us
    all_to_all x1, starting transfers between devices, body(): lax.all_to_all(tile_send.reshape(lats * patches, slots, width), ('lat', '...  14.1 us
    pallas_call x6, Pallas kernels, call(): pl.pallas_call(kernel, out_shape=tuple(outs), in_specs=[ins] * len(operan...  12 us
    ppermute x3, starting transfers between devices, body(): lax.ppermute(pieces[d], 'lat', [(i, i ^ d) for i in range(lats)])  9.58 us
    ppermute x3, waiting for transfers between devices, body(): lax.ppermute(pieces[d], 'lat', [(i, i ^ d) for i in range(lats)])  4.01 us
    all_to_all x1, waiting for transfers between devices, body(): lax.all_to_all(outgoing.reshape(patches, slots, width), 'patch', split_ax...  3.04 us
    ppermute x1, starting transfers between devices, body(): inner = lax.ppermute(inner, 'patch', [(i, i ^ 1) for i in range(patches)])  2.8 us
  transfers between devices with their start and end apart: 7, of which 3 were waited for; matrix products, arithmetic and copies ran while one was open for 0% of the time, Pallas kernels for 4%

profile of v3, /device:TPU:1, one launch (start us, length us, event | category | flops | bytes accessed | tf_op | source)
XLA Modules:
  0.0 84.7 jit_solution(11937498632728210021)
XLA Ops:
  0.6 0.0 copy-start.4
  0.6 1.7 %shard_map.228 = (bf16[256,128]{1,0:T(8,128)(2,1)}, bf16[128,128]{1,0:T(8,128)(2,1)}, bf16[128,128]{1,0:T(8,128)(2,1)}) custom-call(bf16[256,128]{1,0:T(8,128)(2,1)} %nodes_hbm.3, s32[2,128]{1,0:T(2,128)} %bitcast.35), custom_call_target="tpu_custom_call" | custom-call | flops 1048576 | tf_op jit(solution)/shard_map/pallas_call | solution.py:217
  2.3 18.4 %all-to-all-start = ((bf16[128,2,128]{2,1,0:T(2,128)(2,1)}), bf16[128,2,128]{2,1,0:T(2,128)(2,1)S(1)}, u32[]{:S(2)}, u32[]{:S(2)}) async-start(bf16[128,2,128]{2,1,0:T(2,128)(2,1)} %bitcast.26), calls=%async_computation | async-start | bytes 131072 | tf_op jit(solution)/shard_map/all_to_all | solution.py:276
  20.8 2.8 %collective-permute-start = (bf16[128,128]{1,0:T(8,128)(2,1)}, bf16[128,128]{1,0:T(8,128)(2,1)S(1)}, u32[]{:S(2)}, u32[]{:S(2)}) collective-permute-start(bf16[128,128]{1,0:T(8,128)(2,1)} %get-tuple-element.27), channel_id=1, source_target_pairs={{0,4},{4,0},{8,12},{12,8},{16,20},{20,16},{24,28},{28,24},{32,36},... | collective-permute-start | bytes 98312 | tf_op jit(solution)/shard_map/ppermute | solution.py:279
  23.6 2.8 %collective-permute-start.1 = (bf16[128,128]{1,0:T(8,128)(2,1)}, bf16[128,128]{1,0:T(8,128)(2,1)S(1)}, u32[]{:S(2)}, u32[]{:S(2)}) collective-permute-start(bf16[128,128]{1,0:T(8,128)(2,1)} %get-tuple-element.28), channel_id=1, source_target_pairs={{4,8},{8,4},{12,16},{16,12},{20,24},{24,20},{28,32},{32,28},{36,40... | collective-permute-start | bytes 98312 | tf_op jit(solution)/shard_map/ppermute | solution.py:280
  26.4 2.7 %shard_map.229 = (f32[384,512]{1,0:T(8,128)}, bf16[256,512]{1,0:T(8,128)(2,1)}, bf16[128,256]{1,0:T(8,128)(2,1)}, bf16[384,64]{1,0:T(8,128)(2,1)}, bf16[64,384]{1,0:T(8,128)(2,1)}, /*index=5*/f32[8,512]{1,0:T(8,128)}) custom-call(bf16[1536,512]{1,0:T(8,128)(2,1)} %refs_2_.3, bf16[256,512]{1,0:T(8,128)(2,1)} %refs_8_.1, bf16[128,512]{1,0:T(8,128)(2,1)} %refs_9_.1, ...), custom_call_target="tpu_custom_call" | custom-call | flops 201326592 | tf_op jit(solution)/shard_map/pallas_call | solution.py:217
  29.1 0.0 copy-start
  29.1 0.0 copy-start.1
  29.1 0.0 copy-start.2
  29.1 0.0 copy-start.3
  29.1 0.0 copy-start.5
  29.1 0.0 copy-start.6
  29.2 0.0 copy-start.7
  29.2 0.0 copy-start.8
  29.2 0.0 copy-start.9
  29.2 3.0 %all-to-all-done = bf16[128,2,128]{2,1,0:T(2,128)(2,1)S(1)} async-done(((bf16[128,2,128]{2,1,0:T(2,128)(2,1)}), bf16[128,2,128]{2,1,0:T(2,128)(2,1)S(1)}, u32[]{:S(2)}, u32[]{:S(2)}) %all-to-all-start) | async-done | bytes 65568 | tf_op jit(solution)/shard_map/all_to_all | solution.py:276
  32.2 0.0 collective-permute-done.inner_hbm
  32.2 0.0 collective-permute-done.1.outer_hbm
  32.2 0.0 copy-done.4
  32.2 1.2 %shard_map.230 = bf16[4,768,128]{2,1,0:T(8,128)(2,1)S(1)} custom-call(bf16[256,128]{1,0:T(8,128)(2,1)S(1)} %copy-done.4, bf16[128,128]{1,0:T(8,128)(2,1)S(1)} %collective-permute-done.inner_hbm, bf16[128,128]{1,0:T(8,128)(2,1)S(1)} %collective-permute-done.1.outer_hbm, bf16[256,128]{1,0:T(8,128)(2,1)S(1)} %bitcast.24), custom_call_target="tpu_custom_call" | custom-call | tf_op jit(solution)/shard_map/pallas_call | solution.py:217
  33.4 14.5 %all_to_all.15.refs_0_ = bf16[4,768,128]{2,1,0:T(8,128)(2,1)} all-to-all(bf16[4,768,128]{2,1,0:T(8,128)(2,1)S(1)} %shard_map.230), channel_id=1, replica_groups=mesh['patch'=128,'lat'=4] {'lat'}, dimensions={0} | all-to-all | bytes 1572864 | tf_op jit(solution)/shard_map/all_to_all | solution.py:311
  48.0 0.0 copy-done
  48.0 0.0 copy-done.1
  48.0 0.0 copy-done.2
  48.0 0.0 copy-done.3
  48.0 0.0 copy-done.5
  48.0 0.0 copy-done.6
  48.0 0.0 copy-done.7
  48.0 0.0 copy-done.8
  48.1 0.0 copy-done.9
  48.1 5.1 %shard_map.231 = (bf16[256,512]{1,0:T(8,128)(2,1)}, bf16[128,512]{1,0:T(8,128)(2,1)}, bf16[4,256,128]{2,1,0:T(8,128)(2,1)}, bf16[64,128]{1,0:T(8,128)(2,1)S(1)},...) custom-call(bf16[4,768,128]{2,1,0:T(8,128)(2,1)} %all_to_all.15.refs_0_, ...), custom_call_target="tpu_custom_call" | custom-call | flops 1006632960 | tf_op jit(solution)/shard_map/pallas_call | solution.py:217
  53.1 14.1 %all-to-all-start.2 = ((bf16[512,2,128]{2,1,0:T(2,128)(2,1)}), bf16[512,2,128]{2,1,0:T(2,128)(2,1)S(1)}, u32[]{:S(2)}, u32[]{:S(2)}) async-start(bf16[512,2,128]{2,1,0:T(2,128)(2,1)} %bitcast.19), calls=%async_computation.2 | async-start | bytes 524288 | tf_op jit(solution)/shard_map/all_to_all | solution.py:332
  67.3 3.3 %collective-permute-start.2 = (bf16[64,128]{1,0:T(8,128)(2,1)S(1)}, bf16[64,128]{1,0:T(8,128)(2,1)S(1)}, u32[]{:S(2)}, u32[]{:S(2)}) collective-permute-start(bf16[64,128]{1,0:T(8,128)(2,1)S(1)} %get-tuple-element.46), channel_id=1, source_target_pairs={{0,1},{1,0},{2,3},{3,2},{4,5},{5,4},{6,7},{7,6},{8,9},{9,8},{10,11... | collective-permute-start | bytes 49160 | tf_op jit(solution)/shard_map/ppermute | solution.py:336
  70.6 4.3 %collective-permute-start.3 = (bf16[64,128]{1,0:T(8,128)(2,1)S(1)}, bf16[64,128]{1,0:T(8,128)(2,1)S(1)}, u32[]{:S(2)}, u32[]{:S(2)}) collective-permute-start(bf16[64,128]{1,0:T(8,128)(2,1)S(1)} %get-tuple-element.47), channel_id=1, source_target_pairs={{0,2},{1,3},{2,0},{3,1},{4,6},{5,7},{6,4},{7,5},{8,10},{9,11},{10,... | collective-permute-start | bytes 49160 | tf_op jit(solution)/shard_map/ppermute | solution.py:336
  74.9 2.0 %collective-permute-start.4 = (bf16[64,128]{1,0:T(8,128)(2,1)S(1)}, bf16[64,128]{1,0:T(8,128)(2,1)S(1)}, u32[]{:S(2)}, u32[]{:S(2)}) collective-permute-start(bf16[64,128]{1,0:T(8,128)(2,1)S(1)} %get-tuple-element.48), channel_id=1, source_target_pairs={{0,3},{1,2},{2,1},{3,0},{4,7},{5,6},{6,5},{7,4},{8,11},{9,10},{10,... | collective-permute-start | bytes 49160 | tf_op jit(solution)/shard_map/ppermute | solution.py:336
  76.9 0.0 collective-permute-done.2.refs_1_
  76.9 0.0 collective-permute-done.3.refs_2_
  76.9 4.0 %collective-permute-done.4.refs_3_ = bf16[64,128]{1,0:T(8,128)(2,1)S(1)} collective-permute-done((bf16[64,128]{1,0:T(8,128)(2,1)S(1)}, bf16[64,128]{1,0:T(8,128)(2,1)S(1)}, u32[]{:S(2)}, u32[]{:S(2)}) %collective-permute-start.4) | collective-permute-done | bytes 16416 | tf_op jit(solution)/shard_map/ppermute | solution.py:336
  80.9 0.6 shard_map.232
  81.5 2.5 %all-to-all-done.2 = bf16[512,2,128]{2,1,0:T(2,128)(2,1)S(1)} async-done(((bf16[512,2,128]{2,1,0:T(2,128)(2,1)}), bf16[512,2,128]{2,1,0:T(2,128)(2,1)S(1)}, u32[]{:S(2)}, u32[]{:S(2)}) %all-to-all-start.2) | async-done | bytes 262176 | tf_op jit(solution)/shard_map/all_to_all | solution.py:332
  84.0 0.7 shard_map.233
Async XLA Ops:
  0.6 31.6 %copy-start.4 = (bf16[256,128]{1,0:T(8,128)(2,1)S(1)}, bf16[256,128]{1,0:T(8,128)(2,1)}, u32[]{:S(2)}) copy-start(bf16[256,128]{1,0:T(8,128)(2,1)} %nodes_hbm.3) | copy-start | bytes 196612
  2.3 29.9 %all-to-all-start = ((bf16[128,2,128]{2,1,0:T(2,128)(2,1)}), bf16[128,2,128]{2,1,0:T(2,128)(2,1)S(1)}, u32[]{:S(2)}, u32[]{:S(2)}) async-start(bf16[128,2,128]{2,1,0:T(2,128)(2,1)} %bitcast.26), calls=%async_computation | async-start | bytes 131072 | tf_op jit(solution)/shard_map/all_to_all | solution.py:276
  20.8 11.5 %collective-permute-start = (bf16[128,128]{1,0:T(8,128)(2,1)}, bf16[128,128]{1,0:T(8,128)(2,1)S(1)}, u32[]{:S(2)}, u32[]{:S(2)}) collective-permute-start(bf16[128,128]{1,0:T(8,128)(2,1)} %get-tuple-element.27), channel_id=1, source_target_pairs={{0,4},{4,0},{8,12},{12,8},{16,20},{20,16},{24,28},{28,24},{32,36},... | collective-permute-start | bytes 98312 | tf_op jit(solution)/shard_map/ppermute | solution.py:279
  23.6 8.6 %collective-permute-start.1 = (bf16[128,128]{1,0:T(8,128)(2,1)}, bf16[128,128]{1,0:T(8,128)(2,1)S(1)}, u32[]{:S(2)}, u32[]{:S(2)}) collective-permute-start(bf16[128,128]{1,0:T(8,128)(2,1)} %get-tuple-element.28), channel_id=1, source_target_pairs={{4,8},{8,4},{12,16},{16,12},{20,24},{24,20},{28,32},{32,28},{36,40... | collective-permute-start | bytes 98312 | tf_op jit(solution)/shard_map/ppermute | solution.py:280
  29.1 18.9 %copy-start = (bf16[256,512]{1,0:T(8,128)(2,1)S(1)}, bf16[256,512]{1,0:T(8,128)(2,1)}, u32[]{:S(2)}) copy-start(bf16[256,512]{1,0:T(8,128)(2,1)} %refs_8_.1) | copy-start | bytes 786436
  29.1 18.9 %copy-start.1 = (bf16[512,512]{1,0:T(8,128)(2,1)S(1)}, bf16[512,512]{1,0:T(8,128)(2,1)}, u32[]{:S(2)}) copy-start(bf16[512,512]{1,0:T(8,128)(2,1)} %refs_7_.1) | copy-start | bytes 1572868
  29.1 18.9 %copy-start.2 = (bf16[128,512]{1,0:T(8,128)(2,1)S(1)}, bf16[128,512]{1,0:T(8,128)(2,1)}, u32[]{:S(2)}) copy-start(bf16[128,512]{1,0:T(8,128)(2,1)} %refs_9_.1) | copy-start | bytes 393220
  29.1 18.9 %copy-start.3 = (bf16[256,512]{1,0:T(8,128)(2,1)S(1)}, bf16[256,512]{1,0:T(8,128)(2,1)}, u32[]{:S(2)}) copy-start(bf16[256,512]{1,0:T(8,128)(2,1)} %get-tuple-element.37.refs_1_) | copy-start | bytes 786436
  29.1 18.9 %copy-start.5 = (bf16[384,64]{1,0:T(8,128)(2,1)S(1)}, bf16[384,64]{1,0:T(8,128)(2,1)}, u32[]{:S(2)}) copy-start(bf16[384,64]{1,0:T(8,128)(2,1)} %get-tuple-element.38.refs_3_) | copy-start | bytes 147460
  29.1 18.9 %copy-start.6 = (bf16[128,256]{1,0:T(8,128)(2,1)S(1)}, bf16[128,256]{1,0:T(8,128)(2,1)}, u32[]{:S(2)}) copy-start(bf16[128,256]{1,0:T(8,128)(2,1)} %get-tuple-element.40.refs_5_) | copy-start | bytes 196612
  29.2 18.9 %copy-start.7 = (bf16[64,384]{1,0:T(8,128)(2,1)S(1)}, bf16[64,384]{1,0:T(8,128)(2,1)}, u32[]{:S(2)}) copy-start(bf16[64,384]{1,0:T(8,128)(2,1)} %get-tuple-element.42.refs_10_) | copy-start | bytes 147460
  29.2 18.9 %copy-start.8 = (f32[8,512]{1,0:T(8,128)S(1)}, f32[8,512]{1,0:T(8,128)}, u32[]{:S(2)}) copy-start(f32[8,512]{1,0:T(8,128)} %get-tuple-element.41.refs_6_) | copy-start | bytes 49156
  29.2 18.9 %copy-start.9 = (s32[1,128,2]{1,2,0:T(2,128)S(1)}, s32[1,128,2]{1,2,0:T(2,128)}, u32[]{:S(2)}) copy-start(s32[1,128,2]{1,2,0:T(2,128)} %param.29) | copy-start | bytes 3076
  53.1 30.9 %all-to-all-start.2 = ((bf16[512,2,128]{2,1,0:T(2,128)(2,1)}), bf16[512,2,128]{2,1,0:T(2,128)(2,1)S(1)}, u32[]{:S(2)}, u32[]{:S(2)}) async-start(bf16[512,2,128]{2,1,0:T(2,128)(2,1)} %bitcast.19), calls=%async_computation.2 | async-start | bytes 524288 | tf_op jit(solution)/shard_map/all_to_all | solution.py:332
  67.3 9.6 %collective-permute-start.2 = (bf16[64,128]{1,0:T(8,128)(2,1)S(1)}, bf16[64,128]{1,0:T(8,128)(2,1)S(1)}, u32[]{:S(2)}, u32[]{:S(2)}) collective-permute-start(bf16[64,128]{1,0:T(8,128)(2,1)S(1)} %get-tuple-element.46), channel_id=1, source_target_pairs={{0,1},{1,0},{2,3},{3,2},{4,5},{5,4},{6,7},{7,6},{8,9},{9,8},{10,11... | collective-permute-start | bytes 49160 | tf_op jit(solution)/shard_map/ppermute | solution.py:336
  70.6 6.3 %collective-permute-start.3 = (bf16[64,128]{1,0:T(8,128)(2,1)S(1)}, bf16[64,128]{1,0:T(8,128)(2,1)S(1)}, u32[]{:S(2)}, u32[]{:S(2)}) collective-permute-start(bf16[64,128]{1,0:T(8,128)(2,1)S(1)} %get-tuple-element.47), channel_id=1, source_target_pairs={{0,2},{1,3},{2,0},{3,1},{4,6},{5,7},{6,4},{7,5},{8,10},{9,11},{10,... | collective-permute-start | bytes 49160 | tf_op jit(solution)/shard_map/ppermute | solution.py:336
  74.9 6.0 %collective-permute-start.4 = (bf16[64,128]{1,0:T(8,128)(2,1)S(1)}, bf16[64,128]{1,0:T(8,128)(2,1)S(1)}, u32[]{:S(2)}, u32[]{:S(2)}) collective-permute-start(bf16[64,128]{1,0:T(8,128)(2,1)S(1)} %get-tuple-element.48), channel_id=1, source_target_pairs={{0,3},{1,2},{2,1},{3,0},{4,7},{5,6},{6,5},{7,4},{8,11},{9,10},{10,... | collective-permute-start | bytes 49160 | tf_op jit(solution)/shard_map/ppermute | solution.py:336

commit v4 on v2

--- a/solution.py
+++ b/solution.py
@@ -9,7 +9,7 @@
 
 HALO = 128
 COARSE = 16
-LIMITS = {"far": 56, "early": 52, "pack": 52, "main": 52, "tile": 8}
+LIMITS = {"far": 56, "early": 56, "pack": 52, "main": 51, "tile": 8}
 LANES = 128
 F32 = jnp.float32
 BF16 = jnp.bfloat16
@@ -46,12 +46,16 @@
     return jnp.where(places == index_column, 1.0, 0.0).astype(BF16)
 
 
+def shift(power):
+    return power.bit_length() - 1
+
+
 def spread(index_rows, repeat):
     shape = (LANES * repeat, LANES)
     line = lax.broadcasted_iota(jnp.int32, shape, 0)
     patch = lax.broadcasted_iota(jnp.int32, shape, 1)
-    here = lax.div(line, repeat) == patch
-    odd = lax.rem(line, 2) == 1
+    here = (line >> shift(repeat)) == patch
+    odd = (line & 1) == 1
     values = jnp.where(odd, index_rows[1:2].astype(F32), index_rows[0:1].astype(F32))
     return jnp.sum(jnp.where(here, values, 0.0), axis=1, keepdims=True)
 
@@ -184,6 +188,11 @@
 def tile_kernel(rows_ref, index_ref, out_ref):
     hot = pick(spread(index_ref[...], 2), rows_ref.shape[0])
     out_ref[...] = matmul(hot, rows_ref[...]).astype(BF16)
+
+
+def out_kernel(rows_ref, arrived_ref, rows_out, tiles_out):
+    rows_out[...] = rows_ref[...]
+    tiles_out[...] = arrived_ref[...]
 
 
 VMEM = pl.BlockSpec(memory_space=pltpu.VMEM)
@@ -256,17 +265,6 @@
     ).reshape(far, width)
     inner = lax.ppermute(inner, "patch", [(i, i ^ 1) for i in range(patches)])
     outer = lax.ppermute(outer, "patch", [(i, ((i + 1) ^ 1) - 1) for i in range(1, patches - 1)] + [(0, patches - 1), (patches - 1, 0)])
-    (packed,) = call(
-        pack_kernel,
-        [nodes, inner, outer, arrived],
-        [shape((lats, near + far, width))],
-        LIMITS["pack"],
-        0,
-        [DMA((4 * lats,))],
-        out_specs=[ANY],
-    )
-    full = lax.all_to_all(packed, "lat", split_axis=0, concat_axis=0, tiled=True)
-
     vectors = [v.reshape(1, latent) for v in (edge_b_out, edge_gain, edge_shift, node_b_in, node_b_out, node_gain, node_shift)]
     ints = [v.reshape(-1, LANES) for v in (short_send, short_recv, long_send, long_recv)]
     sources = [edge_w_in, short_edges, long_edges, edge_b_in.reshape(1, latent), *ints, *vectors]
@@ -285,6 +283,20 @@
         2 * edges * latent * latent,
         [pltpu.VMEM((latent, latent), BF16)] + like(sources[1:]) + [DMA((len(sources),))],
     )
+    arrived, pre, send_hot, far_hot, recv_hot, recv_cold, vec = lax.optimization_barrier(
+        (arrived, pre, send_hot, far_hot, recv_hot, recv_cold, vec)
+    )
+    (packed,) = call(
+        pack_kernel,
+        [nodes, inner, outer, arrived],
+        [shape((lats, near + far, width))],
+        LIMITS["pack"],
+        0,
+        [DMA((4 * lats,))],
+        out_specs=[ANY],
+    )
+    full = lax.all_to_all(packed, "lat", split_axis=0, concat_axis=0, tiled=True)
+
     sources = [full, send_hot, edge_w_in, recv_hot, pre, far_hot, vec, edge_w_out, short_edges, long_edges, recv_cold]
     sources += [node_w_in, node_w_out]
     places = [pltpu.VMEM((near + far, latent), BF16)] + like(sources[1:])
@@ -311,6 +323,9 @@
         tile_send.reshape(patches, slots, width), "patch", split_axis=0, concat_axis=0, tiled=True
     ).reshape(far, width)
 
+    node_rows, tiles = call(
+        out_kernel, [node_rows, tiles], [shape((rows, width)), shape((far, width))], 8, 2 * far * far * width, ins=VMEM
+    )
     return (short_new, long_new, node_rows, tiles)
 
 

time: 87.7 us -> 84.8 us (0.967)
  blocking collectives: 30.7 us -> 46 us
  waiting for transfers between devices: 14.7 us -> 3.03 us
  starting transfers between devices: 28.2 us -> 24 us
  local copies, waits for them, and re-layouts: 4 us -> 0.06 us
  Pallas kernels: 8.74 us -> 10.4 us
    all_to_all x0 -> x1, blocking collectives: none -> 14.4 us  [body(): lax.all_to_all(packed, 'lat', split_axis=0, concat_axis=0, tiled=True)]
    all_to_all x1 -> x0, waiting for transfers between devices: 8.91 us -> none  [body(): lax.all_to_all(packed, 'lat', split_axis=0, concat_axis=0, tiled=True)]
    all_to_all x1 -> x0, starting transfers between devices: 4.15 us -> none  [body(): lax.all_to_all(packed, 'lat', split_axis=0, concat_axis=0, tiled=True)]
    unnamed x42 -> x22, local copies, waits for them, and re-layouts: 4 us -> 0.06 us
    ppermute x1, waiting for transfers between devices: 3 us -> 0.01 us  [body(): lax.ppermute(outer, 'patch', [(i, (i + 1 ^ 1) - 1) for i in range(1, patc...]
    pallas_call x5 -> x6, Pallas kernels: 8.74 us -> 10.4 us  [call(): pl.pallas_call(kernel, out_shape=tuple(outs), in_specs=[ins] * len(operan...]
  transfers between devices with their start and end apart: 4 -> 3, of which waited for: 3 -> 1; matrix products, arithmetic and copies ran while one was open for 0% -> 0% of each run, Pallas kernels for 2% -> 3%
where the time goes in v4:
time: 84.8 us; the launch traced here: 84.4 us
  blocking collectives  46 us (54%)
  starting transfers between devices  24 us (28%)
  Pallas kernels  10.4 us (12%)
  waiting for transfers between devices  3.03 us (4%)
    all_to_all x1, blocking collectives, body(): lax.all_to_all(tile_send.reshape(patches, slots, width), 'patch', split_a...  24.7 us
    all_to_all x1, starting transfers between devices, body(): lax.all_to_all(outgoing.reshape(patches, slots, width), 'patch', split_ax...  18.4 us
    all_to_all x1, blocking collectives, body(): lax.all_to_all(packed, 'lat', split_axis=0, concat_axis=0, tiled=True)  14.4 us
    pallas_call x6, Pallas kernels, call(): pl.pallas_call(kernel, out_shape=tuple(outs), in_specs=[ins] * len(operan...  10.4 us
    all_to_all x1, blocking collectives, body(): lax.all_to_all(own_new, 'lat', split_axis=0, concat_axis=0, tiled=True)  6.84 us
    all_to_all x1, waiting for transfers between devices, body(): lax.all_to_all(outgoing.reshape(patches, slots, width), 'patch', split_ax...  3.02 us
    ppermute x1, starting transfers between devices, body(): inner = lax.ppermute(inner, 'patch', [(i, i ^ 1) for i in range(patches)])  2.8 us
    ppermute x1, starting transfers between devices, body(): lax.ppermute(outer, 'patch', [(i, (i + 1 ^ 1) - 1) for i in range(1, patc...  2.8 us
  transfers between devices with their start and end apart: 3, of which 1 were waited for; matrix products, arithmetic and copies ran while one was open for 0% of the time, Pallas kernels for 3%

profile of v4, /device:TPU:1, one launch (start us, length us, event | category | flops | bytes accessed | tf_op | source)
XLA Modules:
  0.0 84.4 jit_solution(3725188898391585025)
XLA Ops:
  0.6 0.0 copy-start.5
  0.6 1.7 %shard_map.228 = (bf16[256,128]{1,0:T(8,128)(2,1)}, bf16[128,128]{1,0:T(8,128)(2,1)}, bf16[128,128]{1,0:T(8,128)(2,1)}) custom-call(bf16[256,128]{1,0:T(8,128)(2,1)} %nodes_hbm.3, s32[2,128]{1,0:T(2,128)} %bitcast.38), custom_call_target="tpu_custom_call" | custom-call | flops 1048576 | tf_op jit(solution)/shard_map/pallas_call | solution.py:204
  2.3 18.4 %all-to-all-start = ((bf16[128,2,128]{2,1,0:T(2,128)(2,1)}), bf16[128,2,128]{2,1,0:T(2,128)(2,1)S(1)}, u32[]{:S(2)}, u32[]{:S(2)}) async-start(bf16[128,2,128]{2,1,0:T(2,128)(2,1)} %bitcast.29), calls=%async_computation | async-start | bytes 131072 | tf_op jit(solution)/shard_map/all_to_all | solution.py:263
  20.8 2.8 %collective-permute-start = (bf16[128,128]{1,0:T(8,128)(2,1)}, bf16[128,128]{1,0:T(8,128)(2,1)S(1)}, u32[]{:S(2)}, u32[]{:S(2)}) collective-permute-start(bf16[128,128]{1,0:T(8,128)(2,1)} %get-tuple-element.25), channel_id=1, source_target_pairs={{0,4},{4,0},{8,12},{12,8},{16,20},{20,16},{24,28},{28,24},{32,36},... | collective-permute-start | bytes 98312 | tf_op jit(solution)/shard_map/ppermute | solution.py:266
  23.6 2.8 %collective-permute-start.1 = (bf16[128,128]{1,0:T(8,128)(2,1)}, bf16[128,128]{1,0:T(8,128)(2,1)S(1)}, u32[]{:S(2)}, u32[]{:S(2)}) collective-permute-start(bf16[128,128]{1,0:T(8,128)(2,1)} %get-tuple-element.26), channel_id=1, source_target_pairs={{4,8},{8,4},{12,16},{16,12},{20,24},{24,20},{28,32},{32,28},{36,40... | collective-permute-start | bytes 98312 | tf_op jit(solution)/shard_map/ppermute | solution.py:267
  26.4 2.7 %shard_map.229 = (f32[384,512]{1,0:T(8,128)}, bf16[256,512]{1,0:T(8,128)(2,1)}, bf16[128,256]{1,0:T(8,128)(2,1)}, bf16[384,64]{1,0:T(8,128)(2,1)}, bf16[64,384]{1,0:T(8,128)(2,1)}, /*index=5*/f32[8,512]{1,0:T(8,128)}) custom-call(bf16[1536,512]{1,0:T(8,128)(2,1)} %refs_2_.3, bf16[256,512]{1,0:T(8,128)(2,1)} %refs_8_.1, bf16[128,512]{1,0:T(8,128)(2,1)} %refs_9_.1, ...), custom_call_target="tpu_custom_call" | custom-call | flops 201326592 | tf_op jit(solution)/shard_map/pallas_call | solution.py:204
  29.1 0.0 copy-start
  29.1 0.0 copy-start.1
  29.1 0.0 copy-start.2
  29.1 0.0 copy-start.3
  29.1 0.0 copy-start.4
  29.2 0.0 copy-start.6
  29.2 0.0 copy-start.7
  29.2 0.0 copy-start.8
  29.2 0.0 copy-start.9
  29.2 3.0 %all-to-all-done = bf16[128,2,128]{2,1,0:T(2,128)(2,1)S(1)} async-done(((bf16[128,2,128]{2,1,0:T(2,128)(2,1)}), bf16[128,2,128]{2,1,0:T(2,128)(2,1)S(1)}, u32[]{:S(2)}, u32[]{:S(2)}) %all-to-all-start) | async-done | bytes 65568 | tf_op jit(solution)/shard_map/all_to_all | solution.py:263
  32.2 0.0 collective-permute-done.inner_hbm
  32.2 0.0 collective-permute-done.1.outer_hbm
  32.2 0.0 copy-done.5
  32.2 1.2 %shard_map.230 = bf16[4,768,128]{2,1,0:T(8,128)(2,1)S(1)} custom-call(bf16[256,128]{1,0:T(8,128)(2,1)S(1)} %copy-done.5, bf16[128,128]{1,0:T(8,128)(2,1)S(1)} %collective-permute-done.inner_hbm, bf16[128,128]{1,0:T(8,128)(2,1)S(1)} %collective-permute-done.1.outer_hbm, bf16[256,128]{1,0:T(8,128)(2,1)S(1)} %bitcast.27), custom_call_target="tpu_custom_call" | custom-call | tf_op jit(solution)/shard_map/pallas_call | solution.py:204
  33.4 14.4 %all_to_all.20.refs_0_ = bf16[4,768,128]{2,1,0:T(8,128)(2,1)S(1)} all-to-all(bf16[4,768,128]{2,1,0:T(8,128)(2,1)S(1)} %shard_map.230), channel_id=1, replica_groups=mesh['patch'=128,'lat'=4] {'lat'}, dimensions={0} | all-to-all | bytes 1572864 | tf_op jit(solution)/shard_map/all_to_all | solution.py:298
  47.9 0.0 copy-done
  47.9 0.0 copy-done.1
  47.9 0.0 copy-done.2
  47.9 0.0 copy-done.3
  47.9 0.0 copy-done.4
  47.9 0.0 copy-done.6
  47.9 0.0 copy-done.7
  47.9 0.0 copy-done.8
  47.9 0.0 copy-done.9
  47.9 0.0 copy-start.10
  48.0 3.9 %shard_map.231 = (bf16[256,512]{1,0:T(8,128)(2,1)}, bf16[128,512]{1,0:T(8,128)(2,1)}, bf16[4,64,128]{2,1,0:T(8,128)(2,1)S(1)}) custom-call(bf16[4,768,128]{2,1,0:T(8,128)(2,1)S(1)} %all_to_all.20.refs_0_, bf16[256,512]{1,0:T(8,128)(2,1)S(1)} %copy-done.4, bf16[1536,512]{1,0:T(8,128)(2,1)} %refs_2_.3, bf16[384,64]{1,0:T(8,128)(2,1)S(1)} %copy-done.6, ...), custom_call_target="tpu_custom_call" | custom-call | flops 1006632960 | tf_op jit(solution)/shard_map/pallas_call | solution.py:204
  51.9 6.8 %all_to_all.21 = bf16[4,64,128]{2,1,0:T(8,128)(2,1)S(1)} all-to-all(bf16[4,64,128]{2,1,0:T(8,128)(2,1)S(1)} %get-tuple-element.43), channel_id=1, replica_groups=mesh['patch'=128,'lat'=4] {'lat'}, dimensions={0} | all-to-all | bytes 131072 | tf_op jit(solution)/shard_map/all_to_all | solution.py:313
  58.8 0.0 copy-done.10
  58.8 0.2 shard_map.232
  59.0 24.7 %all_to_all.22 = bf16[128,2,128]{2,1,0:T(2,128)(2,1)S(1)} all-to-all(bf16[128,2,128]{2,1,0:T(2,128)(2,1)S(1)} %bitcast.26), channel_id=1, replica_groups=mesh['patch'=128,'lat'=4] {'patch'}, dimensions={0} | all-to-all | bytes 131072 | tf_op jit(solution)/shard_map/all_to_all | solution.py:322
  83.7 0.7 shard_map.233
Async XLA Ops:
  0.6 31.6 %copy-start.5 = (bf16[256,128]{1,0:T(8,128)(2,1)S(1)}, bf16[256,128]{1,0:T(8,128)(2,1)}, u32[]{:S(2)}) copy-start(bf16[256,128]{1,0:T(8,128)(2,1)} %nodes_hbm.3) | copy-start | bytes 196612
  2.3 29.9 %all-to-all-start = ((bf16[128,2,128]{2,1,0:T(2,128)(2,1)}), bf16[128,2,128]{2,1,0:T(2,128)(2,1)S(1)}, u32[]{:S(2)}, u32[]{:S(2)}) async-start(bf16[128,2,128]{2,1,0:T(2,128)(2,1)} %bitcast.29), calls=%async_computation | async-start | bytes 131072 | tf_op jit(solution)/shard_map/all_to_all | solution.py:263
  20.8 11.5 %collective-permute-start = (bf16[128,128]{1,0:T(8,128)(2,1)}, bf16[128,128]{1,0:T(8,128)(2,1)S(1)}, u32[]{:S(2)}, u32[]{:S(2)}) collective-permute-start(bf16[128,128]{1,0:T(8,128)(2,1)} %get-tuple-element.25), channel_id=1, source_target_pairs={{0,4},{4,0},{8,12},{12,8},{16,20},{20,16},{24,28},{28,24},{32,36},... | collective-permute-start | bytes 98312 | tf_op jit(solution)/shard_map/ppermute | solution.py:266
  23.6 8.6 %collective-permute-start.1 = (bf16[128,128]{1,0:T(8,128)(2,1)}, bf16[128,128]{1,0:T(8,128)(2,1)S(1)}, u32[]{:S(2)}, u32[]{:S(2)}) collective-permute-start(bf16[128,128]{1,0:T(8,128)(2,1)} %get-tuple-element.26), channel_id=1, source_target_pairs={{4,8},{8,4},{12,16},{16,12},{20,24},{24,20},{28,32},{32,28},{36,40... | collective-permute-start | bytes 98312 | tf_op jit(solution)/shard_map/ppermute | solution.py:267
  29.1 18.8 %copy-start = (bf16[256,512]{1,0:T(8,128)(2,1)S(1)}, bf16[256,512]{1,0:T(8,128)(2,1)}, u32[]{:S(2)}) copy-start(bf16[256,512]{1,0:T(8,128)(2,1)} %refs_8_.1) | copy-start | bytes 786436
  29.1 18.8 %copy-start.1 = (bf16[512,512]{1,0:T(8,128)(2,1)S(1)}, bf16[512,512]{1,0:T(8,128)(2,1)}, u32[]{:S(2)}) copy-start(bf16[512,512]{1,0:T(8,128)(2,1)} %refs_7_.1) | copy-start | bytes 1572868
  29.1 18.8 %copy-start.2 = (bf16[512,512]{1,0:T(8,128)(2,1)S(1)}, bf16[512,512]{1,0:T(8,128)(2,1)}, u32[]{:S(2)}) copy-start(bf16[512,512]{1,0:T(8,128)(2,1)} %refs_12_.1) | copy-start | bytes 1572868
  29.1 18.8 %copy-start.3 = (bf16[128,512]{1,0:T(8,128)(2,1)S(1)}, bf16[128,512]{1,0:T(8,128)(2,1)}, u32[]{:S(2)}) copy-start(bf16[128,512]{1,0:T(8,128)(2,1)} %refs_9_.1) | copy-start | bytes 393220
  29.1 18.7 %copy-start.4 = (bf16[256,512]{1,0:T(8,128)(2,1)S(1)}, bf16[256,512]{1,0:T(8,128)(2,1)}, u32[]{:S(2)}) copy-start(bf16[256,512]{1,0:T(8,128)(2,1)} %get-tuple-element.35.refs_1_) | copy-start | bytes 786436
  29.2 18.7 %copy-start.6 = (bf16[384,64]{1,0:T(8,128)(2,1)S(1)}, bf16[384,64]{1,0:T(8,128)(2,1)}, u32[]{:S(2)}) copy-start(bf16[384,64]{1,0:T(8,128)(2,1)} %get-tuple-element.36.refs_3_) | copy-start | bytes 147460
  29.2 18.7 %copy-start.7 = (bf16[128,256]{1,0:T(8,128)(2,1)S(1)}, bf16[128,256]{1,0:T(8,128)(2,1)}, u32[]{:S(2)}) copy-start(bf16[128,256]{1,0:T(8,128)(2,1)} %get-tuple-element.38.refs_5_) | copy-start | bytes 196612
  29.2 18.7 %copy-start.8 = (bf16[64,384]{1,0:T(8,128)(2,1)S(1)}, bf16[64,384]{1,0:T(8,128)(2,1)}, u32[]{:S(2)}) copy-start(bf16[64,384]{1,0:T(8,128)(2,1)} %get-tuple-element.40.refs_10_) | copy-start | bytes 147460
  29.2 18.7 %copy-start.9 = (f32[8,512]{1,0:T(8,128)S(1)}, f32[8,512]{1,0:T(8,128)}, u32[]{:S(2)}) copy-start(f32[8,512]{1,0:T(8,128)} %get-tuple-element.39.refs_6_) | copy-start | bytes 49156
  47.9 10.8 %copy-start.10 = (s32[1,128,2]{1,2,0:T(2,128)S(1)}, s32[1,128,2]{1,2,0:T(2,128)}, u32[]{:S(2)}) copy-start(s32[1,128,2]{1,2,0:T(2,128)} %param.29) | copy-start | bytes 3076

commit v5 on v4

--- a/solution.py
+++ b/solution.py
@@ -162,20 +162,20 @@
         matmul(far_hot[...], full[near:, :]).astype(BF16),
     )
     received = matmul(recv_hot[...], own).astype(BF16)
-    ready(w_in, pre, vec, w_out, short, long)
+    ready(w_in, pre, vec, w_out, short, long, recv_cold, node_w, node_w_out)
     b_out, gain, shift, node_b, node_b_out, node_gain, node_shift = (vec[i : i + 1, :] for i in range(7))
-    parts = ((0, shorts, short, short_new_hbm), (shorts, pre.shape[0], long, long_new_hbm))
+    sent = jnp.concatenate(sents, axis=0)
+    edges = jnp.concatenate([short[...], long[...]], axis=0)
+    own_pre = matmul(own, node_w[:latent, :]) + node_b
+    before = pre[...] + matmul(sent, w_in[:latent, :]) + matmul(received, w_in[latent:, :])
+    output = matmul(silu(before).astype(BF16), w_out[...]) + b_out
+    new_edges[...] = (edges.astype(F32) + norm_rows(output, gain, shift)).astype(BF16)
     stores = []
-    for i, (low, high, edges, out_hbm) in enumerate(parts):
-        before = pre[low:high, :] + matmul(sents[i], w_in[:latent, :]) + matmul(received[low:high], w_in[latent:, :])
-        output = matmul(silu(before).astype(BF16), w_out[...]) + b_out
-        new = edges[...].astype(F32) + norm_rows(output, gain, shift)
-        new_edges[low:high, :] = new.astype(BF16)
+    for i, (low, high, out_hbm) in enumerate(((0, shorts, short_new_hbm), (shorts, pre.shape[0], long_new_hbm))):
         stores.append(pltpu.make_async_copy(new_edges.at[low:high], out_hbm, sems.at[count + chunks + i]))
         stores[-1].start()
-    ready(recv_cold, node_w, node_w_out)
     aggregate = matmul(recv_cold[...], new_edges[...]).astype(BF16)
-    node_pre = matmul(own, node_w[:latent, :]) + matmul(aggregate, node_w[latent:, :]) + node_b
+    node_pre = own_pre + matmul(aggregate, node_w[latent:, :])
     node_out = matmul(silu(node_pre).astype(BF16), node_w_out[...]) + node_b_out
     new = own.astype(F32) + norm_rows(node_out, node_gain, node_shift)
     new = new.astype(BF16)

time: 84.8 us -> 85.1 us (level)
  no operation moved by 1% of the time
where the time goes in v5:
time: 85.1 us; the launch traced here: 84.7 us
  blocking collectives  46 us (54%)
  starting transfers between devices  24 us (28%)
  Pallas kernels  10.8 us (13%)
  waiting for transfers between devices  3.03 us (4%)
    all_to_all x1, blocking collectives, body(): lax.all_to_all(tile_send.reshape(patches, slots, width), 'patch', split_a...  24.7 us
    all_to_all x1, starting transfers between devices, body(): lax.all_to_all(outgoing.reshape(patches, slots, width), 'patch', split_ax...  18.4 us
    all_to_all x1, blocking collectives, body(): lax.all_to_all(packed, 'lat', split_axis=0, concat_axis=0, tiled=True)  14.4 us
    pallas_call x6, Pallas kernels, call(): pl.pallas_call(kernel, out_shape=tuple(outs), in_specs=[ins] * len(operan...  10.8 us
    all_to_all x1, blocking collectives, body(): lax.all_to_all(own_new, 'lat', split_axis=0, concat_axis=0, tiled=True)  6.84 us
    all_to_all x1, waiting for transfers between devices, body(): lax.all_to_all(outgoing.reshape(patches, slots, width), 'patch', split_ax...  3.02 us
    ppermute x1, starting transfers between devices, body(): inner = lax.ppermute(inner, 'patch', [(i, i ^ 1) for i in range(patches)])  2.8 us
    ppermute x1, starting transfers between devices, body(): lax.ppermute(outer, 'patch', [(i, (i + 1 ^ 1) - 1) for i in range(1, patc...  2.8 us
  transfers between devices with their start and end apart: 3, of which 1 were waited for; matrix products, arithmetic and copies ran while one was open for 0% of the time, Pallas kernels for 3%

profile of v5, /device:TPU:1, one launch (start us, length us, event | category | flops | bytes accessed | tf_op | source)
XLA Modules:
  0.0 84.7 jit_solution(11089722448561423756)
XLA Ops:
  0.6 0.0 copy-start.5
  0.6 1.7 %shard_map.228 = (bf16[256,128]{1,0:T(8,128)(2,1)}, bf16[128,128]{1,0:T(8,128)(2,1)}, bf16[128,128]{1,0:T(8,128)(2,1)}) custom-call(bf16[256,128]{1,0:T(8,128)(2,1)} %nodes_hbm.3, s32[2,128]{1,0:T(2,128)} %bitcast.38), custom_call_target="tpu_custom_call" | custom-call | flops 1048576 | tf_op jit(solution)/shard_map/pallas_call | solution.py:204
  2.3 18.4 %all-to-all-start = ((bf16[128,2,128]{2,1,0:T(2,128)(2,1)}), bf16[128,2,128]{2,1,0:T(2,128)(2,1)S(1)}, u32[]{:S(2)}, u32[]{:S(2)}) async-start(bf16[128,2,128]{2,1,0:T(2,128)(2,1)} %bitcast.29), calls=%async_computation | async-start | bytes 131072 | tf_op jit(solution)/shard_map/all_to_all | solution.py:263
  20.8 2.8 %collective-permute-start = (bf16[128,128]{1,0:T(8,128)(2,1)}, bf16[128,128]{1,0:T(8,128)(2,1)S(1)}, u32[]{:S(2)}, u32[]{:S(2)}) collective-permute-start(bf16[128,128]{1,0:T(8,128)(2,1)} %get-tuple-element.25), channel_id=1, source_target_pairs={{0,4},{4,0},{8,12},{12,8},{16,20},{20,16},{24,28},{28,24},{32,36},... | collective-permute-start | bytes 98312 | tf_op jit(solution)/shard_map/ppermute | solution.py:266
  23.6 2.8 %collective-permute-start.1 = (bf16[128,128]{1,0:T(8,128)(2,1)}, bf16[128,128]{1,0:T(8,128)(2,1)S(1)}, u32[]{:S(2)}, u32[]{:S(2)}) collective-permute-start(bf16[128,128]{1,0:T(8,128)(2,1)} %get-tuple-element.26), channel_id=1, source_target_pairs={{4,8},{8,4},{12,16},{16,12},{20,24},{24,20},{28,32},{32,28},{36,40... | collective-permute-start | bytes 98312 | tf_op jit(solution)/shard_map/ppermute | solution.py:267
  26.4 2.7 %shard_map.229 = (f32[384,512]{1,0:T(8,128)}, bf16[256,512]{1,0:T(8,128)(2,1)}, bf16[128,256]{1,0:T(8,128)(2,1)}, bf16[384,64]{1,0:T(8,128)(2,1)}, bf16[64,384]{1,0:T(8,128)(2,1)}, /*index=5*/f32[8,512]{1,0:T(8,128)}) custom-call(bf16[1536,512]{1,0:T(8,128)(2,1)} %refs_2_.3, bf16[256,512]{1,0:T(8,128)(2,1)} %refs_8_.1, bf16[128,512]{1,0:T(8,128)(2,1)} %refs_9_.1, ...), custom_call_target="tpu_custom_call" | custom-call | flops 201326592 | tf_op jit(solution)/shard_map/pallas_call | solution.py:204
  29.1 0.0 copy-start
  29.1 0.0 copy-start.1
  29.1 0.0 copy-start.2
  29.1 0.0 copy-start.3
  29.1 0.0 copy-start.4
  29.2 0.0 copy-start.6
  29.2 0.0 copy-start.7
  29.2 0.0 copy-start.8
  29.2 0.0 copy-start.9
  29.2 3.0 %all-to-all-done = bf16[128,2,128]{2,1,0:T(2,128)(2,1)S(1)} async-done(((bf16[128,2,128]{2,1,0:T(2,128)(2,1)}), bf16[128,2,128]{2,1,0:T(2,128)(2,1)S(1)}, u32[]{:S(2)}, u32[]{:S(2)}) %all-to-all-start) | async-done | bytes 65568 | tf_op jit(solution)/shard_map/all_to_all | solution.py:263
  32.2 0.0 collective-permute-done.inner_hbm
  32.2 0.0 collective-permute-done.1.outer_hbm
  32.2 0.0 copy-done.5
  32.2 1.2 %shard_map.230 = bf16[4,768,128]{2,1,0:T(8,128)(2,1)S(1)} custom-call(bf16[256,128]{1,0:T(8,128)(2,1)S(1)} %copy-done.5, bf16[128,128]{1,0:T(8,128)(2,1)S(1)} %collective-permute-done.inner_hbm, bf16[128,128]{1,0:T(8,128)(2,1)S(1)} %collective-permute-done.1.outer_hbm, bf16[256,128]{1,0:T(8,128)(2,1)S(1)} %bitcast.27), custom_call_target="tpu_custom_call" | custom-call | tf_op jit(solution)/shard_map/pallas_call | solution.py:204
  33.4 14.4 %all_to_all.20.refs_0_ = bf16[4,768,128]{2,1,0:T(8,128)(2,1)S(1)} all-to-all(bf16[4,768,128]{2,1,0:T(8,128)(2,1)S(1)} %shard_map.230), channel_id=1, replica_groups=mesh['patch'=128,'lat'=4] {'lat'}, dimensions={0} | all-to-all | bytes 1572864 | tf_op jit(solution)/shard_map/all_to_all | solution.py:298
  47.9 0.0 copy-done
  47.9 0.0 copy-done.1
  47.9 0.0 copy-done.2
  47.9 0.0 copy-done.3
  47.9 0.0 copy-done.4
  47.9 0.0 copy-done.6
  47.9 0.0 copy-done.7
  47.9 0.0 copy-done.8
  47.9 0.0 copy-done.9
  47.9 0.0 copy-start.10
  48.0 4.3 %shard_map.231 = (bf16[256,512]{1,0:T(8,128)(2,1)}, bf16[128,512]{1,0:T(8,128)(2,1)}, bf16[4,64,128]{2,1,0:T(8,128)(2,1)S(1)}) custom-call(bf16[4,768,128]{2,1,0:T(8,128)(2,1)S(1)} %all_to_all.20.refs_0_, bf16[256,512]{1,0:T(8,128)(2,1)S(1)} %copy-done.4, bf16[1536,512]{1,0:T(8,128)(2,1)} %refs_2_.3, bf16[384,64]{1,0:T(8,128)(2,1)S(1)} %copy-done.6, ...), custom_call_target="tpu_custom_call" | custom-call | flops 1006632960 | tf_op jit(solution)/shard_map/pallas_call | solution.py:204
  52.2 6.8 %all_to_all.21 = bf16[4,64,128]{2,1,0:T(8,128)(2,1)S(1)} all-to-all(bf16[4,64,128]{2,1,0:T(8,128)(2,1)S(1)} %get-tuple-element.43), channel_id=1, replica_groups=mesh['patch'=128,'lat'=4] {'lat'}, dimensions={0} | all-to-all | bytes 131072 | tf_op jit(solution)/shard_map/all_to_all | solution.py:313
  59.1 0.0 copy-done.10
  59.1 0.2 shard_map.232
  59.3 24.7 %all_to_all.22 = bf16[128,2,128]{2,1,0:T(2,128)(2,1)S(1)} all-to-all(bf16[128,2,128]{2,1,0:T(2,128)(2,1)S(1)} %bitcast.26), channel_id=1, replica_groups=mesh['patch'=128,'lat'=4] {'patch'}, dimensions={0} | all-to-all | bytes 131072 | tf_op jit(solution)/shard_map/all_to_all | solution.py:322
  84.0 0.7 shard_map.233
Async XLA Ops:
  0.6 31.6 %copy-start.5 = (bf16[256,128]{1,0:T(8,128)(2,1)S(1)}, bf16[256,128]{1,0:T(8,128)(2,1)}, u32[]{:S(2)}) copy-start(bf16[256,128]{1,0:T(8,128)(2,1)} %nodes_hbm.3) | copy-start | bytes 196612
  2.3 29.9 %all-to-all-start = ((bf16[128,2,128]{2,1,0:T(2,128)(2,1)}), bf16[128,2,128]{2,1,0:T(2,128)(2,1)S(1)}, u32[]{:S(2)}, u32[]{:S(2)}) async-start(bf16[128,2,128]{2,1,0:T(2,128)(2,1)} %bitcast.29), calls=%async_computation | async-start | bytes 131072 | tf_op jit(solution)/shard_map/all_to_all | solution.py:263
  20.8 11.5 %collective-permute-start = (bf16[128,128]{1,0:T(8,128)(2,1)}, bf16[128,128]{1,0:T(8,128)(2,1)S(1)}, u32[]{:S(2)}, u32[]{:S(2)}) collective-permute-start(bf16[128,128]{1,0:T(8,128)(2,1)} %get-tuple-element.25), channel_id=1, source_target_pairs={{0,4},{4,0},{8,12},{12,8},{16,20},{20,16},{24,28},{28,24},{32,36},... | collective-permute-start | bytes 98312 | tf_op jit(solution)/shard_map/ppermute | solution.py:266
  23.6 8.6 %collective-permute-start.1 = (bf16[128,128]{1,0:T(8,128)(2,1)}, bf16[128,128]{1,0:T(8,128)(2,1)S(1)}, u32[]{:S(2)}, u32[]{:S(2)}) collective-permute-start(bf16[128,128]{1,0:T(8,128)(2,1)} %get-tuple-element.26), channel_id=1, source_target_pairs={{4,8},{8,4},{12,16},{16,12},{20,24},{24,20},{28,32},{32,28},{36,40... | collective-permute-start | bytes 98312 | tf_op jit(solution)/shard_map/ppermute | solution.py:267
  29.1 18.8 %copy-start = (bf16[256,512]{1,0:T(8,128)(2,1)S(1)}, bf16[256,512]{1,0:T(8,128)(2,1)}, u32[]{:S(2)}) copy-start(bf16[256,512]{1,0:T(8,128)(2,1)} %refs_8_.1) | copy-start | bytes 786436
  29.1 18.8 %copy-start.1 = (bf16[512,512]{1,0:T(8,128)(2,1)S(1)}, bf16[512,512]{1,0:T(8,128)(2,1)}, u32[]{:S(2)}) copy-start(bf16[512,512]{1,0:T(8,128)(2,1)} %refs_7_.1) | copy-start | bytes 1572868
  29.1 18.8 %copy-start.2 = (bf16[512,512]{1,0:T(8,128)(2,1)S(1)}, bf16[512,512]{1,0:T(8,128)(2,1)}, u32[]{:S(2)}) copy-start(bf16[512,512]{1,0:T(8,128)(2,1)} %refs_12_.1) | copy-start | bytes 1572868
  29.1 18.8 %copy-start.3 = (bf16[128,512]{1,0:T(8,128)(2,1)S(1)}, bf16[128,512]{1,0:T(8,128)(2,1)}, u32[]{:S(2)}) copy-start(bf16[128,512]{1,0:T(8,128)(2,1)} %refs_9_.1) | copy-start | bytes 393220
  29.1 18.7 %copy-start.4 = (bf16[256,512]{1,0:T(8,128)(2,1)S(1)}, bf16[256,512]{1,0:T(8,128)(2,1)}, u32[]{:S(2)}) copy-start(bf16[256,512]{1,0:T(8,128)(2,1)} %get-tuple-element.35.refs_1_) | copy-start | bytes 786436
  29.2 18.7 %copy-start.6 = (bf16[384,64]{1,0:T(8,128)(2,1)S(1)}, bf16[384,64]{1,0:T(8,128)(2,1)}, u32[]{:S(2)}) copy-start(bf16[384,64]{1,0:T(8,128)(2,1)} %get-tuple-element.36.refs_3_) | copy-start | bytes 147460
  29.2 18.7 %copy-start.7 = (bf16[128,256]{1,0:T(8,128)(2,1)S(1)}, bf16[128,256]{1,0:T(8,128)(2,1)}, u32[]{:S(2)}) copy-start(bf16[128,256]{1,0:T(8,128)(2,1)} %get-tuple-element.38.refs_5_) | copy-start | bytes 196612
  29.2 18.7 %copy-start.8 = (bf16[64,384]{1,0:T(8,128)(2,1)S(1)}, bf16[64,384]{1,0:T(8,128)(2,1)}, u32[]{:S(2)}) copy-start(bf16[64,384]{1,0:T(8,128)(2,1)} %get-tuple-element.40.refs_10_) | copy-start | bytes 147460
  29.2 18.7 %copy-start.9 = (f32[8,512]{1,0:T(8,128)S(1)}, f32[8,512]{1,0:T(8,128)}, u32[]{:S(2)}) copy-start(f32[8,512]{1,0:T(8,128)} %get-tuple-element.39.refs_6_) | copy-start | bytes 49156
  47.9 11.1 %copy-start.10 = (s32[1,128,2]{1,2,0:T(2,128)S(1)}, s32[1,128,2]{1,2,0:T(2,128)}, u32[]{:S(2)}) copy-start(s32[1,128,2]{1,2,0:T(2,128)} %param.29) | copy-start | bytes 3076
